TPU v7x, 32 devices: a whole 2x2x4 slice. The times are simulated.
32 devices in a mesh: ens: 2 (over y), lat: 16 (over z, x, core).
Axes of the slice: x: 2, y: 2, z: 4, core: 2. Of those that a mesh axis runs over, the one named last changes fastest.
Arguments:
- signal: bfloat16 [32, 1440, 256], P(('ens', 'lat')), parts along dimension 0, may hold values from -6 to 6
- cotangent: bfloat16 [32, 1440, 256], P(('ens', 'lat')), parts along dimension 0, may hold values from -6 to 6
- weights: bfloat16 [2304, 256], replicated, may hold values from -0.125 to 0.125
- first_row: int32 [16], replicated, may hold values from -2 to -1, as said below
- last_row: int32 [16], replicated, may hold values from 1 to 2, as said below
- lon_reach: int32 [16], replicated, may hold values from 1 to 3, as said below
- basis_index: int32 [16, 5, 7], replicated, may hold values from 0 to 8
- quad_weight: float32 [16, 5, 7], replicated, may hold values from 0.2 to 1
Outputs:
- output: bfloat16 [32, 1440, 256], P(('ens', 'lat')), parts along dimension 0
- signal_grad: bfloat16 [32, 1440, 256], P(('ens', 'lat')), parts along dimension 0
- weight_grad: float32 [4608, 256], P(('ens', 'lat')), parts along dimension 0
There are 2 independent parts, one for each index of `ens`. A program takes and returns all parts, laid end to end along the dimension named above; an argument that names none is the same for every part. Nothing has to cross between parts.
Inputs may be any that keep to these rules, and one draw needn't show every extreme that they name: Rows within 2 of either end of the grid have first_row = -2. Rows within 2 of either end of the grid have last_row = 2. Rows within 2 of either end of the grid have lon_reach = 3.
All inputs are finite; a program needn't handle non-finite values.
Results may differ from a plain program's by a relative error of at most 0.0058.
Values may be sent and summed in bfloat16 or wider, within the bound.
No kernel may reach another device: no remote copies, remote signals or barrier semaphores. Data moves between devices by JAX's collectives and lax.ppermute only.
A program may use at most 384 MiB of HBM per device.

v0:
```python
import functools
import math

import jax
import jax.numpy as jnp
from jax import lax
from jax.experimental import pallas as pl
from jax.experimental.pallas import tpu as pltpu
from jax.sharding import PartitionSpec as P

K = 9
HALO = 2
REACH = 3
DEPTH = 2 * HALO + 1
NOFF = 2 * REACH + 1
BLOCK = 32
WINDOW = 48
SHIFT = 8


def band_matrix(backward, meta, first, last, reach, basis, quad, band32, band):
    row, rows = meta[DEPTH], meta[DEPTH + 1]
    band32[...] = jnp.zeros_like(band32)
    shape = band32.shape[1:]
    diagonal = lax.broadcasted_iota(jnp.int32, shape, 1) - lax.broadcasted_iota(jnp.int32, shape, 0)
    for slot in range(DEPTH):
        place = meta[slot]
        source = row + place - HALO if backward else row
        depth = DEPTH - 1 - place if backward else place
        on_grid = (source >= 0) & (source < rows)
        source = jnp.clip(source, 0, rows - 1)
        inside = on_grid & (depth - HALO >= first[source]) & (depth - HALO <= last[source])
        for step in range(NOFF):
            offset = NOFF - 1 - step if backward else step
            at = (source * DEPTH + depth) * NOFF + offset
            kept = inside & (abs(offset - REACH) <= reach[source])
            value = jnp.where(kept, quad[at], 0.0)
            which = basis[at]
            hit = diagonal == slot * WINDOW + SHIFT - REACH + step
            band32[which] = band32[which] + jnp.where(hit, value, 0.0)
    band[...] = band32[...].reshape(band.shape).astype(band.dtype)


def layer_kernel(backward, *refs):
    scalars, refs = refs[:6], refs[6:]
    slots, refs = refs[:DEPTH], refs[DEPTH:]
    if backward:
        weights, out, band32, band, mixed, shifted = refs
    else:
        weights, turned, out, grad, band32, band, mixed, shifted = refs
    cells, width = out.shape
    band_matrix(backward, *scalars, band32, band)

    def mix(begin, window):
        result = jnp.dot(band[...], window, preferred_element_type=jnp.float32).astype(jnp.bfloat16)
        for k in range(K):
            mixed[pl.ds(begin, BLOCK), k * width : (k + 1) * width] = result[k * BLOCK : (k + 1) * BLOCK]

    @pl.loop(0, cells // BLOCK - 1, unroll=4)
    def _(block):
        begin = pl.multiple_of(block * BLOCK, BLOCK)
        mix(begin, jnp.concatenate([slot[pl.ds(begin, WINDOW), :] for slot in slots], axis=0))

    begin = cells - BLOCK
    pieces = []
    for slot in slots:
        pieces += [slot[begin:, :], slot[: WINDOW - BLOCK, :]]
    mix(begin, jnp.concatenate(pieces, axis=0))

    tile = cells // 5

    @pl.loop(0, 5)
    def _(part):
        begin = pl.multiple_of(part * tile, BLOCK)
        shifted[pl.ds(begin + SHIFT, tile), :] = jnp.dot(
            mixed[pl.ds(begin, tile), :], weights[...], preferred_element_type=jnp.float32
        )

    shifted[:SHIFT] = shifted[cells:]
    for part in range(5):
        out[part * tile : (part + 1) * tile, :] = shifted[part * tile : (part + 1) * tile].astype(out.dtype)
    if not backward:
        for k in range(K):
            term = jnp.dot(
                turned[...], mixed[:, k * width : (k + 1) * width], preferred_element_type=jnp.float32
            )
            grad[k * width : (k + 1) * width, :] = term.T.astype(grad.dtype)


def layer(backward, scalars, slots, weights, turned=None):
    cells, width = slots[0].shape
    outs = [jax.ShapeDtypeStruct((cells, width), jnp.bfloat16)]
    operands = [*slots, weights]
    if not backward:
        outs.append(jax.ShapeDtypeStruct(weights.shape, jnp.bfloat16))
        operands.append(turned)
    smem = pl.BlockSpec(memory_space=pltpu.SMEM)
    vmem = pl.BlockSpec(memory_space=pltpu.VMEM)
    return pl.pallas_call(
        functools.partial(layer_kernel, backward),
        out_shape=outs,
        in_specs=[smem] * 6 + [vmem] * len(operands),
        out_specs=[vmem] * len(outs),
        scratch_shapes=[
            pltpu.VMEM((K, BLOCK, DEPTH * WINDOW), jnp.float32),
            pltpu.VMEM((K * BLOCK, DEPTH * WINDOW), jnp.bfloat16),
            pltpu.VMEM((cells, K * width), jnp.bfloat16),
            pltpu.VMEM((cells + SHIFT, width), jnp.float32),
        ],
        compiler_params=pltpu.CompilerParams(vmem_limit_bytes=40 * 1024 * 1024),
        cost_estimate=pl.CostEstimate(
            flops=2 * cells * K * width * width * (2 if backward else 3),
            bytes_accessed=8 * cells * width * 2,
            transcendentals=0,
        ),
        name="backward_layer" if backward else "forward_layer",
    )(*scalars, *operands)


def shards(signal, cotangent, weights, first_row, last_row, lon_reach, basis_index, quad_weight):
    own_rows, cells, width = signal.shape
    assert own_rows == 1
    devices = lax.axis_size("lat")
    device = lax.axis_index("lat")
    core, side = device % 2, (device // 2) % 2
    across = [(i, i ^ 2) for i in range(devices)]
    cores = [(i, i ^ 1) for i in range(devices)]
    onward = [(i, i + 4) for i in range(devices) if not i & 2 and i + 4 < devices]
    onward += [(i, i - 4) for i in range(devices) if i & 2 and i >= 4]

    def sent(array, pairs):
        return lax.ppermute(array, "lat", pairs)

    meta = jnp.stack(
        [
            jnp.int32(HALO),
            jnp.where(core == 0, HALO + 1, HALO - 1),
            jnp.where(side == 0, 2 * HALO, 0),
            jnp.where(side == 0, 0, 2 * HALO),
            jnp.where(core == 0, HALO - 1, HALO + 1),
            device,
            jnp.int32(devices),
        ]
    ).astype(jnp.int32)
    scalars = [meta, first_row, last_row, lon_reach, basis_index.reshape(-1), quad_weight.reshape(-1)]

    def gathered(row):
        far = sent(row, across)
        beside = sent(row, cores)
        farther = sent(far, onward)
        extra = sent(jnp.where(side == core, far, farther), cores)
        return [row, beside, far, farther, extra]

    signal, cotangent = signal[0], cotangent[0]
    signal_rows = gathered(signal)
    cotangent_rows = gathered(cotangent)
    turned = jnp.roll(cotangent, -SHIFT, 0).T
    weights_back = weights.reshape(K, width, width).swapaxes(1, 2).reshape(K * width, width)

    output, share = layer(False, scalars, signal_rows, weights, turned)
    (signal_grad,) = layer(True, scalars, cotangent_rows, weights_back)

    share = share.reshape(devices, -1, width)
    bit = 1
    while bit < devices:
        part = (device // bit) % 2
        pairs = share.reshape(share.shape[0] // 2, 2, *share.shape[1:])
        kept = lax.dynamic_index_in_dim(pairs, part, 1, keepdims=False)
        given = lax.dynamic_index_in_dim(pairs, 1 - part, 1, keepdims=False)
        arrived = sent(given, [(i, i ^ bit) for i in range(devices)])
        share = kept.astype(jnp.float32) + arrived.astype(jnp.float32)
        bit *= 2
        if bit < devices:
            share = share.astype(jnp.bfloat16)
    weight_grad = share[0] * (1.0 / math.sqrt(devices * cells))
    return output[None], signal_grad[None], weight_grad


def solution(mesh):
    rows = P(("ens", "lat"), None, None)
    return jax.shard_map(
        shards,
        mesh=mesh,
        in_specs=(rows, rows, P(), P(), P(), P(), P(), P()),
        out_specs=(rows, rows, P(("ens", "lat"), None)),
        check_vma=False,
    )
```

profile of v0, /device:TPU:0, one launch (start us, length us, event | category | flops | bytes accessed | tf_op | source)
XLA Modules:
  0.0 107.6 jit_solution(15175958680835137701)
XLA Ops:
  0.6 3.0 %collective-permute-start.1 = (bf16[1440,256]{1,0:T(8,128)(2,1)}, bf16[1440,256]{1,0:T(8,128)(2,1)S(1)}, u32[]{:S(2)}, u32[]{:S(2)}) collective-permute-start(bf16[1440,256]{1,0:T(8,128)(2,1)} %bitcast.43), channel_id=1, source_target_pairs={{0,2},{1,3},{2,0},{3,1},{4,6},{5,7},{6,4},{7,5},{8,10},{9,11},{10,... | collective-permute-start | bytes 2211848 | tf_op jit(solution)/shard_map/ppermute | solution.py:132
  3.6 16.7 %collective-permute-done.1.refs_8_ = bf16[1440,256]{1,0:T(8,128)(2,1)S(1)} collective-permute-done((bf16[1440,256]{1,0:T(8,128)(2,1)}, bf16[1440,256]{1,0:T(8,128)(2,1)S(1)}, u32[]{:S(2)}, u32[]{:S(2)}) %collective-permute-start.1) | collective-permute-done | bytes 737312 | tf_op jit(solution)/shard_map/ppermute | solution.py:132
  20.3 3.8 %collective-permute-start.2 = (bf16[1440,256]{1,0:T(8,128)(2,1)S(1)}, bf16[1440,256]{1,0:T(8,128)(2,1)S(1)}, u32[]{:S(2)}, u32[]{:S(2)}) collective-permute-start(bf16[1440,256]{1,0:T(8,128)(2,1)S(1)} %collective-permute-done.1.refs_8_), channel_id=1, source_target_pairs={{0,4},{1,5},{4,8},{5,9},{8,12},{9,13},{6,2},{7,3},{10,6},{11,7},{1... | collective-permute-start | bytes 2211848 | tf_op jit(solution)/shard_map/ppermute | solution.py:132
  24.1 0.1 collective-permute-start
  24.2 14.7 %collective-permute-done.2.refs_9_ = bf16[1440,256]{1,0:T(8,128)(2,1)S(1)} collective-permute-done((bf16[1440,256]{1,0:T(8,128)(2,1)S(1)}, bf16[1440,256]{1,0:T(8,128)(2,1)S(1)}, u32[]{:S(2)}, u32[]{:S(2)}) %collective-permute-start.2) | collective-permute-done | bytes 737312 | tf_op jit(solution)/shard_map/ppermute | solution.py:132
  38.9 0.0 copy-start.3
  38.9 1.1 %broadcast_select_fusion.1 = bf16[1440,256]{1,0:T(8,128)(2,1)} fusion(bf16[1440,256]{1,0:T(8,128)(2,1)S(1)} %collective-permute-done.1.refs_8_, bf16[1440,256]{1,0:T(8,128)(2,1)S(1)} %collective-permute-done.2.refs_9_, pred[]{:T(512)S(6)} %eq.21), kind=kLoop, calls=%fused_computation.4 | loop fusion | flops 368640 | bytes 2211841 | tf_op jit(solution)/shard_map/jit(_where)/select_n | solution.py:151
  40.0 0.0 collective-permute-start.3
  40.0 2.4 %collective-permute-start.5 = (bf16[1440,256]{1,0:T(8,128)(2,1)}, bf16[1440,256]{1,0:T(8,128)(2,1)S(1)}, u32[]{:S(2)}, u32[]{:S(2)}) collective-permute-start(bf16[1440,256]{1,0:T(8,128)(2,1)} %bitcast.10.refs_6_), channel_id=1, source_target_pairs={{0,2},{1,3},{2,0},{3,1},{4,6},{5,7},{6,4},{7,5},{8,10},{9,11},{10,... | collective-permute-start | bytes 2211848 | tf_op jit(solution)/shard_map/ppermute | solution.py:132
  42.4 0.7 slice.16
  43.1 2.0 %slice.14 = bf16[1,1432,256]{2,1,0:T(8,128)(2,1)} slice(bf16[1,1440,256]{2,1,0:T(8,128)(2,1)} %param.9), slice={[0:1], [8:1440], [0:256]} | slice | bytes 1466368 | tf_op jit(solution)/shard_map/jit(_roll_static)/slice | solution.py:157
  45.1 0.0 copy-done.1
  45.2 0.0 copy-done.3
  45.2 0.1 copy.26
  45.3 0.0 copy-done.11
  45.3 0.1 copy.19
  45.4 0.2 reshape.41.refs_4_
  45.6 0.0 copy-done.12
  45.6 0.1 copy.20
  45.7 0.2 reshape.42.refs_5_
  45.8 1.4 %copy.25 = bf16[1,1432,256]{1,2,0:T(8,128)(2,1)S(1)} copy(bf16[1,1432,256]{2,1,0:T(8,128)(2,1)} %slice.14) | data formatting | bytes 1466368
  47.2 0.0 copy-start
  47.2 0.0 copy-start.8
  47.3 0.0 copy-start.9
  47.3 0.0 copy-start.10
  47.3 0.1 stack.23.refs_0_
  47.4 0.1 maximum_bitcast_fusion.refs_12_
  47.5 0.0 collective-permute-done.refs_7_
  47.5 0.0 copy-start.6
  47.5 0.9 copy-done.6
  48.4 0.0 collective-permute-done.3.refs_10_
  48.4 0.3 copy-done
  48.7 0.0 copy-done.8
  48.7 0.0 copy-done.9
  48.7 0.0 copy-done.10
  48.7 1.1 %copy-done.2 = bf16[1440,256]{1,0:T(8,128)(2,1)S(1)} copy-done((bf16[1440,256]{1,0:T(8,128)(2,1)S(1)}, bf16[1440,256]{1,0:T(8,128)(2,1)}, u32[]{:S(2)}) %copy-start.2) | copy-done | bytes 737304
  49.8 1.1 %copy-done.4 = bf16[1440,256]{1,0:T(8,128)(2,1)S(1)} copy-done((bf16[1440,256]{1,0:T(8,128)(2,1)S(1)}, bf16[1440,256]{1,0:T(8,128)(2,1)}, u32[]{:S(2)}) %copy-start.4) | copy-done | bytes 737304
  50.9 1.1 %copy-done.5 = bf16[1,1440,256]{2,1,0:T(8,128)(2,1)S(1)} copy-done((bf16[1,1440,256]{2,1,0:T(8,128)(2,1)S(1)}, bf16[1,1440,256]{2,1,0:T(8,128)(2,1)}, u32[]{:S(2)}) %copy-start.5) | copy-done | bytes 737304
  52.1 1.1 %copy-done.7 = bf16[1440,256]{1,0:T(8,128)(2,1)S(1)} copy-done((bf16[1440,256]{1,0:T(8,128)(2,1)S(1)}, bf16[1440,256]{1,0:T(8,128)(2,1)}, u32[]{:S(2)}) %copy-start.7) | copy-done | bytes 737304
  53.2 10.7 %forward_layer.1 = (bf16[1440,256]{1,0:T(8,128)(2,1)}, bf16[2304,256]{1,0:T(8,128)(2,1)S(1)}) custom-call(s32[7]{0:T(128)S(1)} %stack.23.refs_0_, s32[16]{0:T(128)S(1)} %copy-done.8, s32[16]{0:T(128)S(1)} %copy-done.9, s32[16]{0:T(128)S(1)} %copy-done.10, s32[560]{0:T(1024)S(1)} %reshape.41.refs_4_, f32[560]{0:T(1024)S(1)} %reshape.42.refs_5_, ...), custom_call_target="tpu_custom_call" | custom-call | flops 5096079360 | bytes 5898240 | tf_op jit(solution)/shard_map/forward_layer/pallas_call | solution.py:99
  63.9 0.9 dynamic-slice_bitcast_fusion
  64.7 0.2 collective-permute-start.8
  65.0 0.0 collective-permute-done.5.refs_8_
  65.0 4.4 %collective-permute-start.6 = (bf16[1440,256]{1,0:T(8,128)(2,1)S(1)}, bf16[1440,256]{1,0:T(8,128)(2,1)}, u32[]{:S(2)}, u32[]{:S(2)}) collective-permute-start(bf16[1440,256]{1,0:T(8,128)(2,1)S(1)} %collective-permute-done.5.refs_8_), channel_id=1, source_target_pairs={{0,4},{1,5},{4,8},{5,9},{8,12},{9,13},{6,2},{7,3},{10,6},{11,7},{1... | collective-permute-start | bytes 2211848 | tf_op jit(solution)/shard_map/ppermute | solution.py:132
  69.3 0.0 collective-permute-start.4
  69.3 0.0 collective-permute-done.8
  69.3 1.2 %fusion = bf16[8,144,256]{2,1,0:T(8,128)(2,1)S(1)} fusion(bf16[8,144,256]{2,1,0:T(8,128)(2,1)} %collective-permute-done.8, bf16[8,2,144,256]{3,2,1,0:T(8,128)(2,1)S(1)} %bitcast.42, s32[]{:T(128)S(6)} %select_n.98), kind=kLoop, calls=%fused_computation.1 | loop fusion | flops 1179648 | bytes 1769476 | tf_op jit(solution)/shard_map/convert_element_type | solution.py:174
  70.6 0.1 collective-permute-start.9
  70.7 13.9 %collective-permute-done.6.refs_9_ = bf16[1440,256]{1,0:T(8,128)(2,1)} collective-permute-done((bf16[1440,256]{1,0:T(8,128)(2,1)S(1)}, bf16[1440,256]{1,0:T(8,128)(2,1)}, u32[]{:S(2)}, u32[]{:S(2)}) %collective-permute-start.6) | collective-permute-done | bytes 737312 | tf_op jit(solution)/shard_map/ppermute | solution.py:132
  84.6 0.9 broadcast_select_fusion
  85.5 0.6 collective-permute-start.7
  86.1 0.0 collective-permute-done.9
  86.2 0.1 fusion.1
  86.2 0.7 dynamic-slice_bitcast_fusion.2
  86.9 2.6 %collective-permute-start.10 = (bf16[2,144,256]{2,1,0:T(8,128)(2,1)}, bf16[2,144,256]{2,1,0:T(8,128)(2,1)}, u32[]{:S(2)}, u32[]{:S(2)}) collective-permute-start(bf16[2,144,256]{2,1,0:T(8,128)(2,1)} %dynamic-slice_bitcast_fusion.2), channel_id=1, source_target_pairs={{0,4},{1,5},{2,6},{3,7},{4,0},{5,1},{6,2},{7,3},{8,12},{9,13},{10,... | collective-permute-start | bytes 442376 | tf_op jit(solution)/shard_map/ppermute | solution.py:132
  89.5 0.7 copy.23
  90.2 3.6 %collective-permute-done.10 = bf16[2,144,256]{2,1,0:T(8,128)(2,1)} collective-permute-done((bf16[2,144,256]{2,1,0:T(8,128)(2,1)}, bf16[2,144,256]{2,1,0:T(8,128)(2,1)}, u32[]{:S(2)}, u32[]{:S(2)}) %collective-permute-start.10) | collective-permute-done | bytes 147488 | tf_op jit(solution)/shard_map/ppermute | solution.py:132
  93.8 1.0 fusion.2
  94.8 2.8 %collective-permute-start.11 = (bf16[1,144,256]{2,1,0:T(8,128)(2,1)S(1)}, bf16[1,144,256]{2,1,0:T(8,128)(2,1)S(1)}, u32[]{:S(2)}, u32[]{:S(2)}) collective-permute-start(bf16[1,144,256]{2,1,0:T(8,128)(2,1)S(1)} %constant_dynamic-slice_fusion), channel_id=1, source_target_pairs={{0,8},{1,9},{2,10},{3,11},{4,12},{5,13},{6,14},{7,15},{8,0},{9,1},... | collective-permute-start | bytes 221192 | tf_op jit(solution)/shard_map/ppermute | solution.py:132
  97.6 0.0 collective-permute-done.4.refs_7_
  97.6 0.0 collective-permute-done.7.refs_10_
  97.6 9.3 %backward_layer.1 = bf16[1440,256]{1,0:T(8,128)(2,1)} custom-call(s32[7]{0:T(128)S(1)} %stack.23.refs_0_, s32[16]{0:T(128)S(1)} %copy-done.8, s32[16]{0:T(128)S(1)} %copy-done.9, s32[16]{0:T(128)S(1)} %copy-done.10, s32[560]{0:T(1024)S(1)} %reshape.41.refs_4_, f32[560]{0:T(1024)S(1)} %reshape.42.refs_5_, bf16[1440,256]{1,0:T(8,128)(2,1)} %bitcast.10.refs_6_, ...), custom_call_target="tpu_custom_call" | custom-call | flops 3397386240 | bytes 5898240 | tf_op jit(solution)/shard_map/backward_layer/pallas_call | solution.py:99
  106.9 0.0 collective-permute-done.11
  106.9 0.7 multiply_bitcast_fusion
  (9 shorter events, 0.1 us)
Async XLA Ops:
  0.6 19.7 %collective-permute-start.1 = (bf16[1440,256]{1,0:T(8,128)(2,1)}, bf16[1440,256]{1,0:T(8,128)(2,1)S(1)}, u32[]{:S(2)}, u32[]{:S(2)}) collective-permute-start(bf16[1440,256]{1,0:T(8,128)(2,1)} %bitcast.43), channel_id=1, source_target_pairs={{0,2},{1,3},{2,0},{3,1},{4,6},{5,7},{6,4},{7,5},{8,10},{9,11},{10,... | collective-permute-start | bytes 2211848 | tf_op jit(solution)/shard_map/ppermute | solution.py:132
  20.3 24.8 %copy-start.1 = (bf16[1440,256]{1,0:T(8,128)(2,1)}, bf16[1440,256]{1,0:T(8,128)(2,1)S(1)}, u32[]{:S(2)}) copy-start(bf16[1440,256]{1,0:T(8,128)(2,1)S(1)} %collective-permute-done.1.refs_8_) | copy-start | bytes 2211844
  20.3 18.6 %collective-permute-start.2 = (bf16[1440,256]{1,0:T(8,128)(2,1)S(1)}, bf16[1440,256]{1,0:T(8,128)(2,1)S(1)}, u32[]{:S(2)}, u32[]{:S(2)}) collective-permute-start(bf16[1440,256]{1,0:T(8,128)(2,1)S(1)} %collective-permute-done.1.refs_8_), channel_id=1, source_target_pairs={{0,4},{1,5},{4,8},{5,9},{8,12},{9,13},{6,2},{7,3},{10,6},{11,7},{1... | collective-permute-start | bytes 2211848 | tf_op jit(solution)/shard_map/ppermute | solution.py:132
  24.1 23.4 %collective-permute-start = (bf16[1440,256]{1,0:T(8,128)(2,1)}, bf16[1440,256]{1,0:T(8,128)(2,1)S(1)}, u32[]{:S(2)}, u32[]{:S(2)}) collective-permute-start(bf16[1440,256]{1,0:T(8,128)(2,1)} %bitcast.44), channel_id=1, source_target_pairs={{0,1},{1,0},{2,3},{3,2},{4,5},{5,4},{6,7},{7,6},{8,9},{9,8},{10,11... | collective-permute-start | bytes 2211848 | tf_op jit(solution)/shard_map/ppermute | solution.py:132
  38.9 6.2 %copy-start.3 = (bf16[1440,256]{1,0:T(8,128)(2,1)}, bf16[1440,256]{1,0:T(8,128)(2,1)S(1)}, u32[]{:S(2)}) copy-start(bf16[1440,256]{1,0:T(8,128)(2,1)S(1)} %collective-permute-done.2.refs_9_) | copy-start | bytes 2211844
  40.0 5.3 %copy-start.11 = (s32[16,5,7]{0,2,1:T(8,128)S(1)}, s32[16,5,7]{0,2,1:T(8,128)}, u32[]{:S(2)}) copy-start(s32[16,5,7]{0,2,1:T(8,128)} %param.14) | copy-start | bytes 6724
  40.0 5.6 %copy-start.12 = (f32[16,5,7]{0,2,1:T(8,128)S(1)}, f32[16,5,7]{0,2,1:T(8,128)}, u32[]{:S(2)}) copy-start(f32[16,5,7]{0,2,1:T(8,128)} %param.15) | copy-start | bytes 6724
  40.0 8.4 %collective-permute-start.3 = (bf16[1440,256]{1,0:T(8,128)(2,1)}, bf16[1440,256]{1,0:T(8,128)(2,1)}, u32[]{:S(2)}, u32[]{:S(2)}) collective-permute-start(bf16[1440,256]{1,0:T(8,128)(2,1)} %broadcast_select_fusion.1), channel_id=1, source_target_pairs={{0,1},{1,0},{2,3},{3,2},{4,5},{5,4},{6,7},{7,6},{8,9},{9,8},{10,11... | collective-permute-start | bytes 2211848 | tf_op jit(solution)/shard_map/ppermute | solution.py:132
  40.0 25.0 %collective-permute-start.5 = (bf16[1440,256]{1,0:T(8,128)(2,1)}, bf16[1440,256]{1,0:T(8,128)(2,1)S(1)}, u32[]{:S(2)}, u32[]{:S(2)}) collective-permute-start(bf16[1440,256]{1,0:T(8,128)(2,1)} %bitcast.10.refs_6_), channel_id=1, source_target_pairs={{0,2},{1,3},{2,0},{3,1},{4,6},{5,7},{6,4},{7,5},{8,10},{9,11},{10,... | collective-permute-start | bytes 2211848 | tf_op jit(solution)/shard_map/ppermute | solution.py:132
  47.2 1.5 %copy-start = (bf16[2304,256]{1,0:T(8,128)(2,1)S(1)}, bf16[2304,256]{1,0:T(8,128)(2,1)}, u32[]{:S(2)}) copy-start(bf16[2304,256]{1,0:T(8,128)(2,1)} %refs_11_.1) | copy-start | bytes 3538948
  47.2 1.5 %copy-start.8 = (s32[16]{0:T(128)S(1)}, s32[16]{0:T(128)}, u32[]{:S(2)}) copy-start(s32[16]{0:T(128)} %refs_1_.3) | copy-start | bytes 196
  47.3 1.4 %copy-start.9 = (s32[16]{0:T(128)S(1)}, s32[16]{0:T(128)}, u32[]{:S(2)}) copy-start(s32[16]{0:T(128)} %refs_2_.3) | copy-start | bytes 196
  47.3 1.4 %copy-start.10 = (s32[16]{0:T(128)S(1)}, s32[16]{0:T(128)}, u32[]{:S(2)}) copy-start(s32[16]{0:T(128)} %refs_3_.3) | copy-start | bytes 196
  47.5 0.9 copy-start.6
  48.7 1.1 %copy-start.2 = (bf16[1440,256]{1,0:T(8,128)(2,1)S(1)}, bf16[1440,256]{1,0:T(8,128)(2,1)}, u32[]{:S(2)}) copy-start(bf16[1440,256]{1,0:T(8,128)(2,1)} %copy-done.1) | copy-start | bytes 2211844
  49.8 1.1 %copy-start.4 = (bf16[1440,256]{1,0:T(8,128)(2,1)S(1)}, bf16[1440,256]{1,0:T(8,128)(2,1)}, u32[]{:S(2)}) copy-start(bf16[1440,256]{1,0:T(8,128)(2,1)} %copy-done.3) | copy-start | bytes 2211844
  50.9 1.1 %copy-start.5 = (bf16[1,1440,256]{2,1,0:T(8,128)(2,1)S(1)}, bf16[1,1440,256]{2,1,0:T(8,128)(2,1)}, u32[]{:S(2)}) copy-start(bf16[1,1440,256]{2,1,0:T(8,128)(2,1)} %param.8) | copy-start | bytes 2211844
  52.1 1.1 %copy-start.7 = (bf16[1440,256]{1,0:T(8,128)(2,1)S(1)}, bf16[1440,256]{1,0:T(8,128)(2,1)}, u32[]{:S(2)}) copy-start(bf16[1440,256]{1,0:T(8,128)(2,1)} %copy-done.6) | copy-start | bytes 2211844
  64.7 4.6 %collective-permute-start.8 = (bf16[8,144,256]{2,1,0:T(8,128)(2,1)}, bf16[8,144,256]{2,1,0:T(8,128)(2,1)}, u32[]{:S(2)}, u32[]{:S(2)}) collective-permute-start(bf16[8,144,256]{2,1,0:T(8,128)(2,1)} %dynamic-slice_bitcast_fusion), channel_id=1, source_target_pairs={{0,1},{1,0},{2,3},{3,2},{4,5},{5,4},{6,7},{7,6},{8,9},{9,8},{10,11... | collective-permute-start | bytes 1769480 | tf_op jit(solution)/shard_map/ppermute | solution.py:132
  65.0 19.7 %collective-permute-start.6 = (bf16[1440,256]{1,0:T(8,128)(2,1)S(1)}, bf16[1440,256]{1,0:T(8,128)(2,1)}, u32[]{:S(2)}, u32[]{:S(2)}) collective-permute-start(bf16[1440,256]{1,0:T(8,128)(2,1)S(1)} %collective-permute-done.5.refs_8_), channel_id=1, source_target_pairs={{0,4},{1,5},{4,8},{5,9},{8,12},{9,13},{6,2},{7,3},{10,6},{11,7},{1... | collective-permute-start | bytes 2211848 | tf_op jit(solution)/shard_map/ppermute | solution.py:132
  69.3 28.3 %collective-permute-start.4 = (bf16[1440,256]{1,0:T(8,128)(2,1)}, bf16[1440,256]{1,0:T(8,128)(2,1)}, u32[]{:S(2)}, u32[]{:S(2)}) collective-permute-start(bf16[1440,256]{1,0:T(8,128)(2,1)} %bitcast.10.refs_6_), channel_id=1, source_target_pairs={{0,1},{1,0},{2,3},{3,2},{4,5},{5,4},{6,7},{7,6},{8,9},{9,8},{10,11... | collective-permute-start | bytes 2211848 | tf_op jit(solution)/shard_map/ppermute | solution.py:132
  70.6 15.6 %collective-permute-start.9 = (bf16[4,144,256]{2,1,0:T(8,128)(2,1)S(1)}, bf16[4,144,256]{2,1,0:T(8,128)(2,1)S(1)}, u32[]{:S(2)}, u32[]{:S(2)}) collective-permute-start(bf16[4,144,256]{2,1,0:T(8,128)(2,1)S(1)} %dynamic-slice_bitcast_fusion.1), channel_id=1, source_target_pairs={{0,2},{1,3},{2,0},{3,1},{4,6},{5,7},{6,4},{7,5},{8,10},{9,11},{10,... | collective-permute-start | bytes 884744 | tf_op jit(solution)/shard_map/ppermute | solution.py:132
  85.5 12.1 %collective-permute-start.7 = (bf16[1440,256]{1,0:T(8,128)(2,1)}, bf16[1440,256]{1,0:T(8,128)(2,1)}, u32[]{:S(2)}, u32[]{:S(2)}) collective-permute-start(bf16[1440,256]{1,0:T(8,128)(2,1)} %broadcast_select_fusion), channel_id=1, source_target_pairs={{0,1},{1,0},{2,3},{3,2},{4,5},{5,4},{6,7},{7,6},{8,9},{9,8},{10,11... | collective-permute-start | bytes 2211848 | tf_op jit(solution)/shard_map/ppermute | solution.py:132
  86.9 6.9 %collective-permute-start.10 = (bf16[2,144,256]{2,1,0:T(8,128)(2,1)}, bf16[2,144,256]{2,1,0:T(8,128)(2,1)}, u32[]{:S(2)}, u32[]{:S(2)}) collective-permute-start(bf16[2,144,256]{2,1,0:T(8,128)(2,1)} %dynamic-slice_bitcast_fusion.2), channel_id=1, source_target_pairs={{0,4},{1,5},{2,6},{3,7},{4,0},{5,1},{6,2},{7,3},{8,12},{9,13},{10,... | collective-permute-start | bytes 442376 | tf_op jit(solution)/shard_map/ppermute | solution.py:132
  94.8 12.1 %collective-permute-start.11 = (bf16[1,144,256]{2,1,0:T(8,128)(2,1)S(1)}, bf16[1,144,256]{2,1,0:T(8,128)(2,1)S(1)}, u32[]{:S(2)}, u32[]{:S(2)}) collective-permute-start(bf16[1,144,256]{2,1,0:T(8,128)(2,1)S(1)} %constant_dynamic-slice_fusion), channel_id=1, source_target_pairs={{0,8},{1,9},{2,10},{3,11},{4,12},{5,13},{6,14},{7,15},{8,0},{9,1},... | collective-permute-start | bytes 221192 | tf_op jit(solution)/shard_map/ppermute | solution.py:132
where the time goes:
time: 108 us
  waiting for transfers between devices  48.9 us (45%)
  Pallas kernels  20 us (19%)
  starting transfers between devices  19.9 us (18%)
  local copies, waits for them, and re-layouts  12.9 us (12%)
  other arithmetic  5.06 us (5%)
    ppermute x12, waiting for transfers between devices, sent(): return lax.ppermute(array, 'lat', pairs)  48.9 us
    pallas_call x2, Pallas kernels, layer(): pl.pallas_call(functools.partial(layer_kernel, backward), out_shape=outs,...  20 us
    ppermute x12, starting transfers between devices, sent(): return lax.ppermute(array, 'lat', pairs)  19.9 us
    unnamed x30, local copies, waits for them, and re-layouts  7.43 us
    slice x2, local copies, waits for them, and re-layouts, shards(): turned = jnp.roll(cotangent, -SHIFT, 0).T  2.74 us
    convert_element_type x3, other arithmetic, shards(): share = share.astype(jnp.bfloat16)  2.26 us
  transfers between devices with their start and end apart: 12, of which 4 were waited for; matrix products, arithmetic and copies ran while one was open for 11% of the time, Pallas kernels for 19%

commit v1 on v0

v1 whole, which is shorter than its diff:
```python
import functools
import math

import jax
import jax.numpy as jnp
from jax import lax
from jax.experimental import pallas as pl
from jax.experimental.pallas import tpu as pltpu
from jax.sharding import PartitionSpec as P

K = 9
HALO = 2
REACH = 3
DEPTH = 2 * HALO + 1
NOFF = 2 * REACH + 1
BLOCK = 32
WINDOW = 48
WRAP = WINDOW - BLOCK
COST = 5_000_000_000
LIMIT = 60
TILES = 5
TIE = 1
LATE = 4
HOLD = True
CUTS_F = ()
CUTS_B = ()
SHIFT = 8


def bands_kernel(meta, first, last, reach, basis, quad, *refs):
    band32 = refs[-1]
    shape = band32.shape[1:]
    diagonal = lax.broadcasted_iota(jnp.int32, shape, 1) - lax.broadcasted_iota(jnp.int32, shape, 0)
    row, rows = meta[DEPTH], meta[DEPTH + 1]
    for backward, band in enumerate(refs[:-1]):
        band32[...] = jnp.zeros_like(band32)
        for slot in range(DEPTH):
            place = meta[slot]
            source = row + place - HALO if backward else row
            depth = DEPTH - 1 - place if backward else place
            on_grid = (source >= 0) & (source < rows)
            source = jnp.clip(source, 0, rows - 1)
            inside = on_grid & (depth - HALO >= first[source]) & (depth - HALO <= last[source])
            for step in range(NOFF):
                offset = NOFF - 1 - step if backward else step
                at = (source * DEPTH + depth) * NOFF + offset
                kept = inside & (abs(offset - REACH) <= reach[source])
                value = jnp.where(kept, quad[at], 0.0)
                which = basis[at]
                hit = diagonal == slot * WINDOW + SHIFT - REACH + step
                band32[which] = band32[which] + jnp.where(hit, value, 0.0)
        band[...] = band32[...].reshape(band.shape).astype(band.dtype)


SMEM = pl.BlockSpec(memory_space=pltpu.SMEM)
VMEM = pl.BlockSpec(memory_space=pltpu.VMEM)
ANY = pl.BlockSpec(memory_space=pl.ANY)
BAND = (K * BLOCK, DEPTH * WINDOW)


def params():
    return pltpu.CompilerParams(vmem_limit_bytes=LIMIT * 1024 * 1024)


def cost(flops):
    return pl.CostEstimate(flops=flops, bytes_accessed=flops // 100, transcendentals=0)


def bands(scalars):
    return pl.pallas_call(
        bands_kernel,
        out_shape=[jax.ShapeDtypeStruct(BAND, jnp.bfloat16)] * 2,
        in_specs=[SMEM] * 6,
        out_specs=[VMEM] * 2,
        scratch_shapes=[pltpu.VMEM((K, BLOCK, DEPTH * WINDOW), jnp.float32)],
        compiler_params=params(),
        name="bands",
    )(*scalars)


def window_copies(counts, pieces, slots, arrived):
    cells = slots.shape[1] - WRAP
    tile = cells // TILES
    groups, used = [], 0
    for part in range(TILES):
        low = part * tile + WRAP if part else 0
        high = (part + 1) * tile + WRAP
        copies = []
        for slot, count in enumerate(counts):
            begin = 0
            moves = []
            for piece in pieces[sum(counts[:slot]) :][:count]:
                end = begin + piece.shape[0]
                first, last = max(low, begin), min(high, end)
                if first < last:
                    moves.append((piece.at[pl.ds(first - begin, last - first)], first))
                if begin == 0 and high > cells:
                    moves.append((piece.at[pl.ds(0, WRAP)], cells))
                begin = end
            for source, at in moves:
                target = slots.at[slot, pl.ds(at, source.shape[0])]
                copies.append(pltpu.make_async_copy(source, target, arrived.at[used]))
                used += 1
        groups.append(copies)
    return groups


def mix(band, slots, mixed, begin, blocks):
    width = slots.shape[2]

    @pl.loop(0, blocks, unroll=3)
    def _(block):
        at = pl.multiple_of(begin + block * BLOCK, BLOCK)
        window = jnp.concatenate([slots[slot, pl.ds(at, WINDOW), :] for slot in range(DEPTH)], axis=0)
        result = jnp.dot(band[...], window, preferred_element_type=jnp.float32).astype(jnp.bfloat16)
        for k in range(K):
            mixed[pl.ds(at, BLOCK), k * width : (k + 1) * width] = result[k * BLOCK : (k + 1) * BLOCK]


def layer_kernel(counts, meta, *refs):
    pieces, refs = refs[: sum(counts)], refs[sum(counts) :]
    *given, mixed, shifted, slots, weights, turned, grad, arrived, fetched = refs
    band, weights_in, *given = given
    turned_in, out, *grads = given if len(given) > 1 else (None, *given)
    cells, width = out.shape
    tile = cells // TILES
    groups = window_copies(counts, pieces, slots, arrived)
    fetches = [pltpu.make_async_copy(weights_in, weights, fetched.at[0])]
    if grads:
        fetches.append(pltpu.make_async_copy(turned_in, turned, fetched.at[1]))
    for copy in groups[0]:
        copy.start()
    for copy in fetches:
        copy.start()
    for copies in groups[1:]:
        for copy in copies:
            copy.start()
    for part in range(TILES):
        for copy in groups[part]:
            copy.wait()
        mix(band, slots, mixed, part * tile, tile // BLOCK)
        if part == 0:
            for copy in fetches:
                copy.wait()
        shifted[part * tile + SHIFT : (part + 1) * tile + SHIFT] = jnp.dot(
            mixed[part * tile : (part + 1) * tile], weights[...], preferred_element_type=jnp.float32
        )
    shifted[:SHIFT] = shifted[cells:]
    for part in range(TILES):
        out[part * tile : (part + 1) * tile, :] = shifted[part * tile : (part + 1) * tile].astype(out.dtype)
    if not grads:
        return
    target = grads[0] if len(grads) == 1 else grad
    for k in range(K):
        term = jnp.dot(turned[...], mixed[:, k * width : (k + 1) * width], preferred_element_type=jnp.float32)
        target[k * width : (k + 1) * width, :] = term.T.astype(grad.dtype)
    if len(grads) == 2:
        core = meta[DEPTH] % 2
        lines = grads[0].shape[1]
        for pair in range(grads[0].shape[0]):
            for which, array in enumerate(grads):
                other = core if which == 0 else 1 - core
                at = pl.multiple_of((2 * pair + other) * lines, 16)
                array[pair] = grad[pl.ds(at, lines), :]


def layer(meta, band, slots, weights, devices, turned=None):
    width = weights.shape[1]
    cells = sum(piece.shape[0] for piece in slots[0])
    counts = tuple(len(slot) for slot in slots)
    pieces = [piece for slot in slots for piece in slot]
    lines = K * width // devices
    outs = [jax.ShapeDtypeStruct((cells, width), jnp.bfloat16)]
    operands = [weights]
    if turned is not None:
        operands.append(turned)
        if lines % 16 == 0:
            outs += [jax.ShapeDtypeStruct((devices // 2, lines, width), jnp.bfloat16)] * 2
        else:
            outs += [jax.ShapeDtypeStruct((K * width, width), jnp.bfloat16)]
    out, *grads = pl.pallas_call(
        functools.partial(layer_kernel, counts),
        out_shape=outs,
        in_specs=[SMEM] + [ANY] * len(pieces) + [VMEM] + [ANY] * len(operands),
        out_specs=[VMEM] * len(outs),
        scratch_shapes=[
            pltpu.VMEM((cells, K * width), jnp.bfloat16),
            pltpu.VMEM((cells + SHIFT, width), jnp.float32),
            pltpu.VMEM((DEPTH, cells + WRAP, width), jnp.bfloat16),
            pltpu.VMEM(weights.shape, jnp.bfloat16),
            pltpu.VMEM((width, cells), jnp.bfloat16),
            pltpu.VMEM((K * width, width), jnp.bfloat16),
            pltpu.SemaphoreType.DMA((TILES * 2 * len(pieces),)),
            pltpu.SemaphoreType.DMA((2,)),
        ],
        compiler_params=params(),
        cost_estimate=cost(COST),
        name="backward_layer" if turned is None else "forward_layer",
    )(meta, *pieces, band, *operands)
    if len(grads) == 1:
        parts = grads[0].reshape(devices // 2, 2, lines, width)
        core = meta[DEPTH] % 2
        grads = [lax.dynamic_index_in_dim(parts, at, 1, keepdims=False) for at in (core, 1 - core)]
    return out, *grads


def shards(signal, cotangent, weights, first_row, last_row, lon_reach, basis_index, quad_weight):
    own_rows, cells, width = signal.shape
    assert own_rows == 1
    devices = lax.axis_size("lat")
    device = lax.axis_index("lat")
    core, side = device % 2, (device // 2) % 2
    across = [(i, i ^ 2) for i in range(devices)]
    cores = [(i, i ^ 1) for i in range(devices)]
    onward = [(i, i + 4) for i in range(devices) if not i & 2 and i + 4 < devices]
    onward += [(i, i - 4) for i in range(devices) if i & 2 and i >= 4]

    def sent(array, pairs):
        return lax.ppermute(array, "lat", pairs)

    meta = jnp.stack(
        [
            jnp.int32(HALO),
            jnp.where(core == 0, HALO + 1, HALO - 1),
            jnp.where(side == 0, 2 * HALO, 0),
            jnp.where(side == 0, 0, 2 * HALO),
            jnp.where(core == 0, HALO - 1, HALO + 1),
            device,
            jnp.int32(devices),
        ]
    ).astype(jnp.int32)
    scalars = [meta, first_row, last_row, lon_reach, basis_index.reshape(-1), quad_weight.reshape(-1)]

    def split(row, cuts):
        edges = [0, *cuts, cells]
        return [row[low:high] for low, high in zip(edges, edges[1:])]

    def swapped(far, farther):
        return [sent(jnp.where(side == core, one, other), cores) for one, other in zip(far, farther)]

    signal, cotangent = signal[0], cotangent[0]
    turned = jnp.roll(cotangent, -SHIFT, 0).T
    weights_back = weights.reshape(K, width, width).swapaxes(1, 2).reshape(K * width, width)

    first_piece, *later = split(signal, CUTS_F)
    signal_far = [sent(first_piece, across)]
    if later:
        signal_far[0], later, cotangent_sent = lax.optimization_barrier((signal_far[0], later, cotangent))
    else:
        cotangent_sent = cotangent
    signal_far += [sent(piece, across) for piece in later]
    cotangent_far = [sent(piece, across) for piece in split(cotangent_sent, CUTS_B)]
    signal_beside, cotangent_beside = sent(signal, cores), sent(cotangent, cores)
    ready = (turned, weights_back, bands(scalars), signal_beside, cotangent_beside)
    signal_far[0], ready = lax.optimization_barrier((signal_far[0], ready))
    turned, weights_back, (band, band_back), signal_beside, cotangent_beside = ready
    signal_farther = [sent(piece, onward) for piece in signal_far]
    cotangent_farther = [sent(piece, onward) for piece in cotangent_far]
    if HOLD:
        signal_farther, _ = lax.optimization_barrier((signal_farther, cotangent_far))
    signal_extra = swapped(signal_far, signal_farther)
    signal_rows = [[signal], [signal_beside], signal_far, signal_farther, signal_extra]
    cotangent_rows = [[cotangent], [cotangent_beside], cotangent_far, cotangent_farther, None]

    output, kept, given = layer(meta, band, signal_rows, weights, devices, turned)
    bit = 1
    while True:
        if bit == TIE:
            given, cotangent_rows[3] = lax.optimization_barrier((given, cotangent_rows[3]))
        arrived = sent(given, [(i, i ^ bit) for i in range(devices)])
        share = kept.astype(jnp.float32) + arrived.astype(jnp.float32)
        bit *= 2
        if bit == devices:
            break
        share = share.astype(jnp.bfloat16)
        if bit == TIE * 2 or TIE == 0 and bit == 2:
            cotangent_rows[4] = swapped(cotangent_far, cotangent_rows[3])
            (signal_grad,) = layer(meta, band_back, cotangent_rows, weights_back, devices)
        if bit == LATE:
            share, signal_grad = lax.optimization_barrier((share, signal_grad))
        parts = share.reshape(share.shape[0] // 2, 2, *share.shape[1:])
        part = (device // bit) % 2
        kept = lax.dynamic_index_in_dim(parts, part, 1, keepdims=False)
        given = lax.dynamic_index_in_dim(parts, 1 - part, 1, keepdims=False)
    weight_grad = share[0] * (1.0 / math.sqrt(devices * cells))
    return output[None], signal_grad[None], weight_grad


def solution(mesh):
    rows = P(("ens", "lat"), None, None)
    return jax.shard_map(
        shards,
        mesh=mesh,
        in_specs=(rows, rows, P(), P(), P(), P(), P(), P()),
        out_specs=(rows, rows, P(("ens", "lat"), None)),
        check_vma=False,
    )
```

time: 108 us -> 89.8 us (0.83)
  waiting for transfers between devices: 48.9 us -> 33 us
  Pallas kernels: 20 us -> 26.2 us
  local copies, waits for them, and re-layouts: 12.9 us -> 7.29 us
  other arithmetic: 5.06 us -> 3.5 us
  starting transfers between devices: 19.9 us -> 18.7 us
    ppermute x12, waiting for transfers between devices: 48.9 us -> 33 us  [sent(): return lax.ppermute(array, 'lat', pairs)]
    pallas_call x2 -> x3, Pallas kernels: 20 us -> 26.2 us  [the longest x2 24.3 us: layer(): pl.pallas_call(functools.partial(layer_kernel, counts), out_shape=outs, i...]
    unnamed x30 -> x20, local copies, waits for them, and re-layouts: 7.43 us -> 1.53 us
    convert_element_type x3, other arithmetic: 2.26 us -> 0.28 us  [shards(): share = share.astype(jnp.bfloat16)]
    squeeze x4 -> x3, local copies, waits for them, and re-layouts: 1.58 us -> 0.06 us  [shards(): given = lax.dynamic_index_in_dim(parts, 1 - part, 1, keepdims=False)]
    ppermute x12, starting transfers between devices: 19.9 us -> 18.7 us  [sent(): return lax.ppermute(array, 'lat', pairs)]
  transfers between devices with their start and end apart: 12 -> 12, of which waited for: 4 -> 7; matrix products, arithmetic and copies ran while one was open for 11% -> 8% of each run, Pallas kernels for 19% -> 29%
where the time goes in v1:
time: 89.8 us; the launch traced here: 89.5 us
  waiting for transfers between devices  33 us (37%)
  Pallas kernels  26.2 us (29%)
  starting transfers between devices  18.7 us (21%)
  local copies, waits for them, and re-layouts  7.29 us (8%)
  other arithmetic  3.5 us (4%)
    ppermute x12, waiting for transfers between devices, sent(): return lax.ppermute(array, 'lat', pairs)  33 us
    pallas_call x2, Pallas kernels, layer(): pl.pallas_call(functools.partial(layer_kernel, counts), out_shape=outs, i...  24.3 us
    ppermute x12, starting transfers between devices, sent(): return lax.ppermute(array, 'lat', pairs)  18.7 us
    slice x2, local copies, waits for them, and re-layouts, shards(): turned = jnp.roll(cotangent, -SHIFT, 0).T  1.98 us
    pallas_call x1, Pallas kernels, bands(): pl.pallas_call(bands_kernel, out_shape=[jax.ShapeDtypeStruct(BAND, jnp.bf...  1.91 us
  transfers between devices with their start and end apart: 12, of which 7 were waited for; matrix products, arithmetic and copies ran while one was open for 8% of the time, Pallas kernels for 29%

profile of v1, /device:TPU:0, one launch (start us, length us, event | category | flops | bytes accessed | tf_op | source)
XLA Modules:
  0.0 89.5 jit_solution(725268407320195999)
XLA Ops:
  0.6 0.0 copy-start.5
  0.6 0.0 copy-start.6
  0.7 3.0 %collective-permute-start = (bf16[1440,256]{1,0:T(8,128)(2,1)}, bf16[1440,256]{1,0:T(8,128)(2,1)}, u32[]{:S(2)}, u32[]{:S(2)}) collective-permute-start(bf16[1440,256]{1,0:T(8,128)(2,1)} %bitcast.44), channel_id=1, source_target_pairs={{0,2},{1,3},{2,0},{3,1},{4,6},{5,7},{6,4},{7,5},{8,10},{9,11},{10,... | collective-permute-start | bytes 2211848 | tf_op jit(solution)/shard_map/ppermute | solution.py:219
  3.7 0.0 collective-permute-start.1
  3.7 0.5 collective-permute-start.2
  4.2 0.1 collective-permute-start.4
  4.2 1.2 %slice.14 = bf16[1,1432,256]{2,1,0:T(8,128)(2,1)S(1)} slice(bf16[1,1440,256]{2,1,0:T(8,128)(2,1)} %param.9), slice={[0:1], [8:1440], [0:256]} | slice | bytes 1466368 | tf_op jit(solution)/shard_map/jit(_roll_static)/slice | solution.py:242
  5.4 0.0 copy-start
  5.5 0.8 slice.16
  6.2 0.0 copy-done.5
  6.2 0.1 copy.17
  6.4 0.7 reshape.41.basis
  7.1 0.0 copy-done.6
  7.1 0.1 copy.18
  7.2 0.7 reshape.42.quad
  8.0 0.3 copy.20
  8.3 0.1 copy.21
  8.4 0.0 copy-done
  8.4 1.5 %copy.16 = bf16[9,256,256]{1,2,0:T(8,128)(2,1)} copy(bf16[9,256,256]{2,1,0:T(8,128)(2,1)S(1)} %bitcast.38) | data formatting | bytes 2359296 | tf_op jit(solution)/shard_map/reshape | solution.py:243
  9.9 0.7 stack.23.meta
  10.6 1.9 %bands.1 = (bf16[288,240]{1,0:T(8,128)(2,1)}, bf16[288,240]{1,0:T(8,128)(2,1)}) custom-call(s32[7]{0:T(128)} %stack.23.meta, s32[16]{0:T(128)} %first.1, s32[16]{0:T(128)} %last.1, s32[16]{0:T(128)} %reach.1, s32[560]{0:T(1024)} %reshape.41.basis, f32[560]{0:T(1024)} %reshape.42.quad), custom_call_target="tpu_custom_call" | custom-call | tf_op jit(solution)/shard_map/bands/pallas_call | solution.py:70
  12.5 1.0 %maximum_bitcast_fusion.refs_7_ = bf16[256,1440]{1,0:T(8,128)(2,1)} fusion(bf16[8,256]{0,1:T(8,128)(2,1)S(1)} %bitcast.43, bf16[1432,256]{0,1:T(8,128)(2,1)S(1)} %bitcast.33), kind=kLoop, calls=%fused_computation.1 | loop fusion | flops 1474560 | bytes 1474560 | tf_op jit(solution)/shard_map/transpose | solution.py:242
  13.5 7.8 %collective-permute-done.refs_2_ = bf16[1440,256]{1,0:T(8,128)(2,1)} collective-permute-done((bf16[1440,256]{1,0:T(8,128)(2,1)}, bf16[1440,256]{1,0:T(8,128)(2,1)}, u32[]{:S(2)}, u32[]{:S(2)}) %collective-permute-start) | collective-permute-done | bytes 737312 | tf_op jit(solution)/shard_map/ppermute | solution.py:219
  21.3 0.0 collective-permute-done.1.refs_1_
  21.3 0.0 collective-permute-done.2.refs_1_
  21.3 4.1 %collective-permute-start.3 = (bf16[1440,256]{1,0:T(8,128)(2,1)}, bf16[1440,256]{1,0:T(8,128)(2,1)S(1)}, u32[]{:S(2)}, u32[]{:S(2)}) collective-permute-start(bf16[1440,256]{1,0:T(8,128)(2,1)} %collective-permute-done.refs_2_), channel_id=1, source_target_pairs={{0,4},{1,5},{4,8},{5,9},{8,12},{9,13},{6,2},{7,3},{10,6},{11,7},{1... | collective-permute-start | bytes 2211848 | tf_op jit(solution)/shard_map/ppermute | solution.py:219
  25.4 10.8 %collective-permute-done.4.refs_2_ = bf16[1440,256]{1,0:T(8,128)(2,1)S(1)} collective-permute-done((bf16[1440,256]{1,0:T(8,128)(2,1)}, bf16[1440,256]{1,0:T(8,128)(2,1)S(1)}, u32[]{:S(2)}, u32[]{:S(2)}) %collective-permute-start.4) | collective-permute-done | bytes 737312 | tf_op jit(solution)/shard_map/ppermute | solution.py:219
  36.2 0.0 copy-start.1
  36.2 3.2 %collective-permute-done.3.refs_3_ = bf16[1440,256]{1,0:T(8,128)(2,1)S(1)} collective-permute-done((bf16[1440,256]{1,0:T(8,128)(2,1)}, bf16[1440,256]{1,0:T(8,128)(2,1)S(1)}, u32[]{:S(2)}, u32[]{:S(2)}) %collective-permute-start.3) | collective-permute-done | bytes 737312 | tf_op jit(solution)/shard_map/ppermute | solution.py:219
  39.4 0.0 copy-start.3
  39.4 1.5 %broadcast_select_fusion.1 = bf16[1440,256]{1,0:T(8,128)(2,1)S(1)} fusion(bf16[1440,256]{1,0:T(8,128)(2,1)} %collective-permute-done.refs_2_, bf16[1440,256]{1,0:T(8,128)(2,1)S(1)} %collective-permute-done.3.refs_3_, pred[]{:T(512)S(6)} %eq.20), kind=kLoop, calls=%fused_computation.3 | loop fusion | flops 368640 | bytes 2211841 | tf_op jit(solution)/shard_map/jit(_where)/select_n | solution.py:239
  40.8 0.1 collective-permute-start.5
  40.9 4.3 %collective-permute-start.6 = (bf16[1440,256]{1,0:T(8,128)(2,1)S(1)}, bf16[1440,256]{1,0:T(8,128)(2,1)S(1)}, u32[]{:S(2)}, u32[]{:S(2)}) collective-permute-start(bf16[1440,256]{1,0:T(8,128)(2,1)S(1)} %collective-permute-done.4.refs_2_), channel_id=1, source_target_pairs={{0,4},{1,5},{4,8},{5,9},{8,12},{9,13},{6,2},{7,3},{10,6},{11,7},{1... | collective-permute-start | bytes 2211848 | tf_op jit(solution)/shard_map/ppermute | solution.py:219
  45.2 0.0 collective-permute-done.5.refs_4_
  45.3 0.0 copy-done.3
  45.3 13.5 %forward_layer.1 = (bf16[1440,256]{1,0:T(8,128)(2,1)}, bf16[8,144,256]{2,1,0:T(8,128)(2,1)}, bf16[8,144,256]{2,1,0:T(8,128)(2,1)}) custom-call(s32[7]{0:T(128)} %stack.23.meta, bf16[1440,256]{1,0:T(8,128)(2,1)} %bitcast.46, bf16[1440,256]{1,0:T(8,128)(2,1)} %collective-permute-done.1.refs_1_, bf16[1440,256]{1,0:T(8,128)(2,1)} %collective-permute-done.refs_2_, ...), custom_call_target="tpu_custom_call" | custom-call | flops 5000000000 | bytes 50000000 | tf_op jit(solution)/shard_map/forward_layer/pallas_call | solution.py:181
  58.8 0.0 copy-start.4
  58.8 2.8 %collective-permute-done.6.refs_3_ = bf16[1440,256]{1,0:T(8,128)(2,1)S(1)} collective-permute-done((bf16[1440,256]{1,0:T(8,128)(2,1)S(1)}, bf16[1440,256]{1,0:T(8,128)(2,1)S(1)}, u32[]{:S(2)}, u32[]{:S(2)}) %collective-permute-start.6) | collective-permute-done | bytes 737312 | tf_op jit(solution)/shard_map/ppermute | solution.py:219
  61.6 0.0 copy-start.2
  61.6 0.0 collective-permute-start.7
  61.6 0.0 copy-done.1
  61.6 0.1 broadcast_select_fusion
  61.7 0.6 collective-permute-start.9
  62.3 1.5 %collective-permute-done.7 = bf16[8,144,256]{2,1,0:T(8,128)(2,1)S(1)} collective-permute-done((bf16[8,144,256]{2,1,0:T(8,128)(2,1)}, bf16[8,144,256]{2,1,0:T(8,128)(2,1)S(1)}, u32[]{:S(2)}, u32[]{:S(2)}) %collective-permute-start.7) | collective-permute-done | bytes 589856 | tf_op jit(solution)/shard_map/ppermute | solution.py:219
  63.8 0.0 copy-done.4
  63.8 0.1 add_convert_fusion
  63.9 0.0 copy-done.2
  64.0 1.1 %collective-permute-start.8 = (bf16[4,144,256]{2,1,0:T(8,128)(2,1)S(1)}, bf16[4,144,256]{2,1,0:T(8,128)(2,1)S(1)}, u32[]{:S(2)}, u32[]{:S(2)}) collective-permute-start(bf16[4,144,256]{2,1,0:T(8,128)(2,1)S(1)} %dynamic-slice_bitcast_fusion), channel_id=1, source_target_pairs={{0,2},{1,3},{2,0},{3,1},{4,6},{5,7},{6,4},{7,5},{8,10},{9,11},{10,... | collective-permute-start | bytes 884744 | tf_op jit(solution)/shard_map/ppermute | solution.py:219
  65.1 0.0 collective-permute-done.9.refs_4_
  65.1 0.0 copy-start.7
  65.1 0.9 copy-done.7
  66.0 10.8 %backward_layer.1 = bf16[1440,256]{1,0:T(8,128)(2,1)} custom-call(s32[7]{0:T(128)} %stack.23.meta, bf16[1440,256]{1,0:T(8,128)(2,1)} %bitcast.42, bf16[1440,256]{1,0:T(8,128)(2,1)} %collective-permute-done.2.refs_1_, bf16[1440,256]{1,0:T(8,128)(2,1)} %copy-done.1, bf16[1440,256]{1,0:T(8,128)(2,1)} %copy-done.2, bf16[1440,256]{1,0:T(8,128)(2,1)} %copy-done.7, ...), custom_call_target="tpu_custom_call" | custom-call | flops 5000000000 | bytes 50000000 | tf_op jit(solution)/shard_map/backward_layer/pallas_call | solution.py:181
  76.7 0.0 collective-permute-done.8
  76.8 0.1 fusion
  76.9 2.1 %collective-permute-start.10 = (bf16[2,144,256]{2,1,0:T(8,128)(2,1)S(1)}, bf16[2,144,256]{2,1,0:T(8,128)(2,1)S(1)}, u32[]{:S(2)}, u32[]{:S(2)}) collective-permute-start(bf16[2,144,256]{2,1,0:T(8,128)(2,1)S(1)} %dynamic-slice_bitcast_fusion.1), channel_id=1, source_target_pairs={{0,4},{1,5},{2,6},{3,7},{4,0},{5,1},{6,2},{7,3},{8,12},{9,13},{10,... | collective-permute-start | bytes 442376 | tf_op jit(solution)/shard_map/ppermute | solution.py:219
  79.0 4.1 %collective-permute-done.10 = bf16[2,144,256]{2,1,0:T(8,128)(2,1)S(1)} collective-permute-done((bf16[2,144,256]{2,1,0:T(8,128)(2,1)S(1)}, bf16[2,144,256]{2,1,0:T(8,128)(2,1)S(1)}, u32[]{:S(2)}, u32[]{:S(2)}) %collective-permute-start.10) | collective-permute-done | bytes 147488 | tf_op jit(solution)/shard_map/ppermute | solution.py:219
  83.2 2.8 %collective-permute-start.11 = (bf16[1,144,256]{2,1,0:T(8,128)(2,1)S(1)}, bf16[1,144,256]{2,1,0:T(8,128)(2,1)S(1)}, u32[]{:S(2)}, u32[]{:S(2)}) collective-permute-start(bf16[1,144,256]{2,1,0:T(8,128)(2,1)S(1)} %constant_dynamic-slice_fusion), channel_id=1, source_target_pairs={{0,8},{1,9},{2,10},{3,11},{4,12},{5,13},{6,14},{7,15},{8,0},{9,1},... | collective-permute-start | bytes 221192 | tf_op jit(solution)/shard_map/ppermute | solution.py:219
  86.0 2.8 %collective-permute-done.11 = bf16[1,144,256]{2,1,0:T(8,128)(2,1)S(1)} collective-permute-done((bf16[1,144,256]{2,1,0:T(8,128)(2,1)S(1)}, bf16[1,144,256]{2,1,0:T(8,128)(2,1)S(1)}, u32[]{:S(2)}, u32[]{:S(2)}) %collective-permute-start.11) | collective-permute-done | bytes 73760 | tf_op jit(solution)/shard_map/ppermute | solution.py:219
  88.8 0.7 multiply_bitcast_fusion
  (4 shorter events, 0.1 us)
Async XLA Ops:
  0.6 5.6 %copy-start.5 = (s32[16,5,7]{0,2,1:T(8,128)S(1)}, s32[16,5,7]{0,2,1:T(8,128)}, u32[]{:S(2)}) copy-start(s32[16,5,7]{0,2,1:T(8,128)} %param.14) | copy-start | bytes 6724
  0.6 6.5 %copy-start.6 = (f32[16,5,7]{0,2,1:T(8,128)S(1)}, f32[16,5,7]{0,2,1:T(8,128)}, u32[]{:S(2)}) copy-start(f32[16,5,7]{0,2,1:T(8,128)} %param.15) | copy-start | bytes 6724
  0.7 20.6 %collective-permute-start = (bf16[1440,256]{1,0:T(8,128)(2,1)}, bf16[1440,256]{1,0:T(8,128)(2,1)}, u32[]{:S(2)}, u32[]{:S(2)}) collective-permute-start(bf16[1440,256]{1,0:T(8,128)(2,1)} %bitcast.44), channel_id=1, source_target_pairs={{0,2},{1,3},{2,0},{3,1},{4,6},{5,7},{6,4},{7,5},{8,10},{9,11},{10,... | collective-permute-start | bytes 2211848 | tf_op jit(solution)/shard_map/ppermute | solution.py:219
  3.7 17.6 %collective-permute-start.1 = (bf16[1440,256]{1,0:T(8,128)(2,1)}, bf16[1440,256]{1,0:T(8,128)(2,1)}, u32[]{:S(2)}, u32[]{:S(2)}) collective-permute-start(bf16[1440,256]{1,0:T(8,128)(2,1)} %bitcast.45), channel_id=1, source_target_pairs={{0,1},{1,0},{2,3},{3,2},{4,5},{5,4},{6,7},{7,6},{8,9},{9,8},{10,11... | collective-permute-start | bytes 2211848 | tf_op jit(solution)/shard_map/ppermute | solution.py:219
  3.7 17.6 %collective-permute-start.2 = (bf16[1440,256]{1,0:T(8,128)(2,1)}, bf16[1440,256]{1,0:T(8,128)(2,1)}, u32[]{:S(2)}, u32[]{:S(2)}) collective-permute-start(bf16[1440,256]{1,0:T(8,128)(2,1)} %bitcast.40), channel_id=1, source_target_pairs={{0,1},{1,0},{2,3},{3,2},{4,5},{5,4},{6,7},{7,6},{8,9},{9,8},{10,11... | collective-permute-start | bytes 2211848 | tf_op jit(solution)/shard_map/ppermute | solution.py:219
  4.2 32.0 %collective-permute-start.4 = (bf16[1440,256]{1,0:T(8,128)(2,1)}, bf16[1440,256]{1,0:T(8,128)(2,1)S(1)}, u32[]{:S(2)}, u32[]{:S(2)}) collective-permute-start(bf16[1440,256]{1,0:T(8,128)(2,1)} %bitcast.41), channel_id=1, source_target_pairs={{0,2},{1,3},{2,0},{3,1},{4,6},{5,7},{6,4},{7,5},{8,10},{9,11},{10,... | collective-permute-start | bytes 2211848 | tf_op jit(solution)/shard_map/ppermute | solution.py:219
  5.4 2.9 %copy-start = (bf16[2304,256]{1,0:T(8,128)(2,1)S(1)}, bf16[2304,256]{1,0:T(8,128)(2,1)}, u32[]{:S(2)}) copy-start(bf16[2304,256]{1,0:T(8,128)(2,1)} %refs_6_.1) | copy-start | bytes 3538948
  21.3 18.1 %collective-permute-start.3 = (bf16[1440,256]{1,0:T(8,128)(2,1)}, bf16[1440,256]{1,0:T(8,128)(2,1)S(1)}, u32[]{:S(2)}, u32[]{:S(2)}) collective-permute-start(bf16[1440,256]{1,0:T(8,128)(2,1)} %collective-permute-done.refs_2_), channel_id=1, source_target_pairs={{0,4},{1,5},{4,8},{5,9},{8,12},{9,13},{6,2},{7,3},{10,6},{11,7},{1... | collective-permute-start | bytes 2211848 | tf_op jit(solution)/shard_map/ppermute | solution.py:219
  36.2 25.4 %copy-start.1 = (bf16[1440,256]{1,0:T(8,128)(2,1)}, bf16[1440,256]{1,0:T(8,128)(2,1)S(1)}, u32[]{:S(2)}) copy-start(bf16[1440,256]{1,0:T(8,128)(2,1)S(1)} %collective-permute-done.4.refs_2_) | copy-start | bytes 2211844
  39.4 5.9 %copy-start.3 = (bf16[1440,256]{1,0:T(8,128)(2,1)}, bf16[1440,256]{1,0:T(8,128)(2,1)S(1)}, u32[]{:S(2)}) copy-start(bf16[1440,256]{1,0:T(8,128)(2,1)S(1)} %collective-permute-done.3.refs_3_) | copy-start | bytes 2211844
  40.8 4.4 %collective-permute-start.5 = (bf16[1440,256]{1,0:T(8,128)(2,1)S(1)}, bf16[1440,256]{1,0:T(8,128)(2,1)}, u32[]{:S(2)}, u32[]{:S(2)}) collective-permute-start(bf16[1440,256]{1,0:T(8,128)(2,1)S(1)} %broadcast_select_fusion.1), channel_id=1, source_target_pairs={{0,1},{1,0},{2,3},{3,2},{4,5},{5,4},{6,7},{7,6},{8,9},{9,8},{10,11... | collective-permute-start | bytes 2211848 | tf_op jit(solution)/shard_map/ppermute | solution.py:219
  40.9 20.7 %collective-permute-start.6 = (bf16[1440,256]{1,0:T(8,128)(2,1)S(1)}, bf16[1440,256]{1,0:T(8,128)(2,1)S(1)}, u32[]{:S(2)}, u32[]{:S(2)}) collective-permute-start(bf16[1440,256]{1,0:T(8,128)(2,1)S(1)} %collective-permute-done.4.refs_2_), channel_id=1, source_target_pairs={{0,4},{1,5},{4,8},{5,9},{8,12},{9,13},{6,2},{7,3},{10,6},{11,7},{1... | collective-permute-start | bytes 2211848 | tf_op jit(solution)/shard_map/ppermute | solution.py:219
  58.8 5.0 %copy-start.4 = (bf16[8,144,256]{2,1,0:T(8,128)(2,1)S(1)}, bf16[8,144,256]{2,1,0:T(8,128)(2,1)}, u32[]{:S(2)}) copy-start(bf16[8,144,256]{2,1,0:T(8,128)(2,1)} %get-tuple-element.28) | copy-start | bytes 1769476
  61.6 2.4 %copy-start.2 = (bf16[1440,256]{1,0:T(8,128)(2,1)}, bf16[1440,256]{1,0:T(8,128)(2,1)S(1)}, u32[]{:S(2)}) copy-start(bf16[1440,256]{1,0:T(8,128)(2,1)S(1)} %collective-permute-done.6.refs_3_) | copy-start | bytes 2211844
  61.6 2.2 %collective-permute-start.7 = (bf16[8,144,256]{2,1,0:T(8,128)(2,1)}, bf16[8,144,256]{2,1,0:T(8,128)(2,1)S(1)}, u32[]{:S(2)}, u32[]{:S(2)}) collective-permute-start(bf16[8,144,256]{2,1,0:T(8,128)(2,1)} %get-tuple-element.30), channel_id=1, source_target_pairs={{0,1},{1,0},{2,3},{3,2},{4,5},{5,4},{6,7},{7,6},{8,9},{9,8},{10,11... | collective-permute-start | bytes 1769480 | tf_op jit(solution)/shard_map/ppermute | solution.py:219
  61.7 3.4 %collective-permute-start.9 = (bf16[1440,256]{1,0:T(8,128)(2,1)S(1)}, bf16[1440,256]{1,0:T(8,128)(2,1)S(1)}, u32[]{:S(2)}, u32[]{:S(2)}) collective-permute-start(bf16[1440,256]{1,0:T(8,128)(2,1)S(1)} %broadcast_select_fusion), channel_id=1, source_target_pairs={{0,1},{1,0},{2,3},{3,2},{4,5},{5,4},{6,7},{7,6},{8,9},{9,8},{10,11... | collective-permute-start | bytes 2211848 | tf_op jit(solution)/shard_map/ppermute | solution.py:219
  64.0 12.8 %collective-permute-start.8 = (bf16[4,144,256]{2,1,0:T(8,128)(2,1)S(1)}, bf16[4,144,256]{2,1,0:T(8,128)(2,1)S(1)}, u32[]{:S(2)}, u32[]{:S(2)}) collective-permute-start(bf16[4,144,256]{2,1,0:T(8,128)(2,1)S(1)} %dynamic-slice_bitcast_fusion), channel_id=1, source_target_pairs={{0,2},{1,3},{2,0},{3,1},{4,6},{5,7},{6,4},{7,5},{8,10},{9,11},{10,... | collective-permute-start | bytes 884744 | tf_op jit(solution)/shard_map/ppermute | solution.py:219
  65.1 0.9 copy-start.7
  76.9 6.3 %collective-permute-start.10 = (bf16[2,144,256]{2,1,0:T(8,128)(2,1)S(1)}, bf16[2,144,256]{2,1,0:T(8,128)(2,1)S(1)}, u32[]{:S(2)}, u32[]{:S(2)}) collective-permute-start(bf16[2,144,256]{2,1,0:T(8,128)(2,1)S(1)} %dynamic-slice_bitcast_fusion.1), channel_id=1, source_target_pairs={{0,4},{1,5},{2,6},{3,7},{4,0},{5,1},{6,2},{7,3},{8,12},{9,13},{10,... | collective-permute-start | bytes 442376 | tf_op jit(solution)/shard_map/ppermute | solution.py:219
  83.2 5.6 %collective-permute-start.11 = (bf16[1,144,256]{2,1,0:T(8,128)(2,1)S(1)}, bf16[1,144,256]{2,1,0:T(8,128)(2,1)S(1)}, u32[]{:S(2)}, u32[]{:S(2)}) collective-permute-start(bf16[1,144,256]{2,1,0:T(8,128)(2,1)S(1)} %constant_dynamic-slice_fusion), channel_id=1, source_target_pairs={{0,8},{1,9},{2,10},{3,11},{4,12},{5,13},{6,14},{7,15},{8,0},{9,1},... | collective-permute-start | bytes 221192 | tf_op jit(solution)/shard_map/ppermute | solution.py:219

commit v2 on v1

--- a/solution.py
+++ b/solution.py
@@ -18,11 +18,12 @@
 WRAP = WINDOW - BLOCK
 COST = 5_000_000_000
 LIMIT = 60
-TILES = 5
+FCOST = 1
+TILES = 3
 TIE = 1
 LATE = 4
 HOLD = True
-CUTS_F = ()
+CUTS_F = (720,)
 CUTS_B = ()
 SHIFT = 8
 
@@ -108,7 +109,7 @@
 def mix(band, slots, mixed, begin, blocks):
     width = slots.shape[2]
 
-    @pl.loop(0, blocks, unroll=3)
+    @pl.loop(0, blocks, unroll=5)
     def _(block):
         at = pl.multiple_of(begin + block * BLOCK, BLOCK)
         window = jnp.concatenate([slots[slot, pl.ds(at, WINDOW), :] for slot in range(DEPTH)], axis=0)
@@ -194,7 +195,7 @@
             pltpu.SemaphoreType.DMA((2,)),
         ],
         compiler_params=params(),
-        cost_estimate=cost(COST),
+        cost_estimate=cost(COST if turned is None else FCOST),
         name="backward_layer" if turned is None else "forward_layer",
     )(meta, *pieces, band, *operands)
     if len(grads) == 1:
@@ -242,18 +243,16 @@
     turned = jnp.roll(cotangent, -SHIFT, 0).T
     weights_back = weights.reshape(K, width, width).swapaxes(1, 2).reshape(K * width, width)
 
-    first_piece, *later = split(signal, CUTS_F)
-    signal_far = [sent(first_piece, across)]
-    if later:
-        signal_far[0], later, cotangent_sent = lax.optimization_barrier((signal_far[0], later, cotangent))
+    signal_far = [sent(piece, across) for piece in split(signal, CUTS_F)]
+    signal_beside, cotangent_beside = sent(signal, cores), sent(cotangent, cores)
+    ready = (turned, weights_back, bands(scalars), meta)
+    if CUTS_F:
+        signal_far[0], cotangent_sent, ready = lax.optimization_barrier((signal_far[0], cotangent, ready))
+        cotangent_far = [sent(piece, across) for piece in split(cotangent_sent, CUTS_B)]
     else:
-        cotangent_sent = cotangent
-    signal_far += [sent(piece, across) for piece in later]
-    cotangent_far = [sent(piece, across) for piece in split(cotangent_sent, CUTS_B)]
-    signal_beside, cotangent_beside = sent(signal, cores), sent(cotangent, cores)
-    ready = (turned, weights_back, bands(scalars), signal_beside, cotangent_beside)
-    signal_far[0], ready = lax.optimization_barrier((signal_far[0], ready))
-    turned, weights_back, (band, band_back), signal_beside, cotangent_beside = ready
+        cotangent_far = [sent(piece, across) for piece in split(cotangent, CUTS_B)]
+        signal_far[0], ready = lax.optimization_barrier((signal_far[0], ready))
+    turned, weights_back, (band, band_back), meta = ready
     signal_farther = [sent(piece, onward) for piece in signal_far]
     cotangent_farther = [sent(piece, onward) for piece in cotangent_far]
     if HOLD:

time: 89.8 us -> 84.6 us (0.942)
  waiting for transfers between devices: 33 us -> 24.7 us
  starting transfers between devices: 18.7 us -> 24.4 us
  Pallas kernels: 26.2 us -> 22.9 us
  local copies, waits for them, and re-layouts: 7.29 us -> 8.23 us
    ppermute x12 -> x15, waiting for transfers between devices: 33 us -> 24.7 us  [sent(): return lax.ppermute(array, 'lat', pairs)]
    ppermute x12 -> x15, starting transfers between devices: 18.7 us -> 24.4 us  [sent(): return lax.ppermute(array, 'lat', pairs)]
    pallas_call x2, Pallas kernels: 24.3 us -> 20.9 us  [layer(): pl.pallas_call(functools.partial(layer_kernel, counts), out_shape=outs, i...]
    slice x0 -> x1, local copies, waits for them, and re-layouts: none -> 2.01 us  [split(): return [row[low:high] for low, high in zip(edges, edges[1:])]]
    slice x2 -> x4, local copies, waits for them, and re-layouts: 1.98 us -> 0.01 us  [shards(): turned = jnp.roll(cotangent, -SHIFT, 0).T]
    unnamed x20 -> x30, local copies, waits for them, and re-layouts: 1.53 us -> 2.47 us
  transfers between devices with their start and end apart: 12 -> 15, of which waited for: 7 -> 10; matrix products, arithmetic and copies ran while one was open for 8% -> 8% of each run, Pallas kernels for 29% -> 27%
where the time goes in v2:
time: 84.6 us; the launch traced here: 84.3 us
  waiting for transfers between devices  24.7 us (29%)
  starting transfers between devices  24.4 us (29%)
  Pallas kernels  22.9 us (27%)
  local copies, waits for them, and re-layouts  8.23 us (10%)
  other arithmetic  3.21 us (4%)
    ppermute x15, waiting for transfers between devices, sent(): return lax.ppermute(array, 'lat', pairs)  24.7 us
    ppermute x15, starting transfers between devices, sent(): return lax.ppermute(array, 'lat', pairs)  24.4 us
    pallas_call x2, Pallas kernels, layer(): pl.pallas_call(functools.partial(layer_kernel, counts), out_shape=outs, i...  20.9 us
    unnamed x30, local copies, waits for them, and re-layouts  2.47 us
    slice x1, local copies, waits for them, and re-layouts, split(): return [row[low:high] for low, high in zip(edges, edges[1:])]  2.01 us
    pallas_call x1, Pallas kernels, bands(): pl.pallas_call(bands_kernel, out_shape=[jax.ShapeDtypeStruct(BAND, jnp.bf...  1.93 us
  transfers between devices with their start and end apart: 15, of which 10 were waited for; matrix products, arithmetic and copies ran while one was open for 8% of the time, Pallas kernels for 27%

profile of v2, /device:TPU:0, one launch (start us, length us, event | category | flops | bytes accessed | tf_op | source)
XLA Modules:
  0.0 84.3 jit_solution(15087530505644453550)
XLA Ops:
  0.6 0.0 copy-start.10
  0.6 2.0 %slice_bitcast_fusion = (bf16[720,256]{1,0:T(8,128)(2,1)}, bf16[720,256]{1,0:T(8,128)(2,1)}) fusion(bf16[1,1440,256]{2,1,0:T(8,128)(2,1)} %param.8), kind=kLoop, calls=%fused_computation.5 | loop fusion | bytes 1474560 | tf_op jit(solution)/shard_map/slice | solution.py:237
  2.7 2.9 %collective-permute-start = (bf16[720,256]{1,0:T(8,128)(2,1)}, bf16[720,256]{1,0:T(8,128)(2,1)S(1)}, u32[]{:S(2)}, u32[]{:S(2)}) collective-permute-start(bf16[720,256]{1,0:T(8,128)(2,1)} %get-tuple-element.40), channel_id=1, source_target_pairs={{0,2},{1,3},{2,0},{3,1},{4,6},{5,7},{6,4},{7,5},{8,10},{9,11},{10,... | collective-permute-start | bytes 1105928 | tf_op jit(solution)/shard_map/ppermute | solution.py:220
  5.6 0.1 collective-permute-start.2
  5.7 0.0 copy-done.10
  5.7 0.1 copy.17
  5.8 0.7 reshape.43.basis
  6.5 0.0 copy-done.11
  6.5 0.1 copy.18
  6.6 0.7 reshape.44.quad
  7.4 0.0 slice-done
  7.4 0.3 copy.20
  7.7 0.0 slice-done.1
  7.7 0.1 copy.21
  7.8 0.0 copy-done
  7.8 1.5 %copy.16 = bf16[9,256,256]{1,2,0:T(8,128)(2,1)} copy(bf16[9,256,256]{2,1,0:T(8,128)(2,1)S(1)} %bitcast.37) | data formatting | bytes 2359296 | tf_op jit(solution)/shard_map/reshape | solution.py:244
  9.4 0.7 stack.23.meta
  10.0 1.9 %bands.1 = (bf16[288,240]{1,0:T(8,128)(2,1)}, bf16[288,240]{1,0:T(8,128)(2,1)}) custom-call(s32[7]{0:T(128)} %stack.23.meta, s32[16]{0:T(128)} %first.1, s32[16]{0:T(128)} %last.1, s32[16]{0:T(128)} %reach.1, s32[560]{0:T(1024)} %reshape.43.basis, f32[560]{0:T(1024)} %reshape.44.quad), custom_call_target="tpu_custom_call" | custom-call | tf_op jit(solution)/shard_map/bands/pallas_call | solution.py:71
  11.9 1.0 %maximum_bitcast_fusion.refs_10_ = bf16[256,1440]{1,0:T(8,128)(2,1)} fusion(bf16[8,256]{0,1:T(8,128)(2,1)S(1)} %bitcast.49, bf16[1432,256]{0,1:T(8,128)(2,1)S(1)} %bitcast.38), kind=kLoop, calls=%fused_computation.1 | loop fusion | flops 1474560 | bytes 1474560 | tf_op jit(solution)/shard_map/transpose | solution.py:243
  12.9 2.3 %collective-permute-done.refs_2_ = bf16[720,256]{1,0:T(8,128)(2,1)S(1)} collective-permute-done((bf16[720,256]{1,0:T(8,128)(2,1)}, bf16[720,256]{1,0:T(8,128)(2,1)S(1)}, u32[]{:S(2)}, u32[]{:S(2)}) %collective-permute-start) | collective-permute-done | bytes 368672 | tf_op jit(solution)/shard_map/ppermute | solution.py:220
  15.2 0.0 copy-done.2
  15.2 2.1 %collective-permute-start.5 = (bf16[1440,256]{1,0:T(8,128)(2,1)S(1)}, bf16[1440,256]{1,0:T(8,128)(2,1)}, u32[]{:S(2)}, u32[]{:S(2)}) collective-permute-start(bf16[1440,256]{1,0:T(8,128)(2,1)S(1)} %bitcast.42), channel_id=1, source_target_pairs={{0,2},{1,3},{2,0},{3,1},{4,6},{5,7},{6,4},{7,5},{8,10},{9,11},{10,... | collective-permute-start | bytes 2211848 | tf_op jit(solution)/shard_map/ppermute | solution.py:220
  17.3 3.5 %collective-permute-start.3 = (bf16[720,256]{1,0:T(8,128)(2,1)S(1)}, bf16[720,256]{1,0:T(8,128)(2,1)S(1)}, u32[]{:S(2)}, u32[]{:S(2)}) collective-permute-start(bf16[720,256]{1,0:T(8,128)(2,1)S(1)} %collective-permute-done.refs_2_), channel_id=1, source_target_pairs={{0,4},{1,5},{4,8},{5,9},{8,12},{9,13},{6,2},{7,3},{10,6},{11,7},{1... | collective-permute-start | bytes 1105928 | tf_op jit(solution)/shard_map/ppermute | solution.py:220
  20.8 2.3 %collective-permute-done.2.refs_3_ = bf16[720,256]{1,0:T(8,128)(2,1)S(1)} collective-permute-done((bf16[720,256]{1,0:T(8,128)(2,1)}, bf16[720,256]{1,0:T(8,128)(2,1)S(1)}, u32[]{:S(2)}, u32[]{:S(2)}) %collective-permute-start.2) | collective-permute-done | bytes 368672 | tf_op jit(solution)/shard_map/ppermute | solution.py:220
  23.1 4.1 %collective-permute-start.4 = (bf16[720,256]{1,0:T(8,128)(2,1)S(1)}, bf16[720,256]{1,0:T(8,128)(2,1)S(1)}, u32[]{:S(2)}, u32[]{:S(2)}) collective-permute-start(bf16[720,256]{1,0:T(8,128)(2,1)S(1)} %collective-permute-done.2.refs_3_), channel_id=1, source_target_pairs={{0,4},{1,5},{4,8},{5,9},{8,12},{9,13},{6,2},{7,3},{10,6},{11,7},{1... | collective-permute-start | bytes 1105928 | tf_op jit(solution)/shard_map/ppermute | solution.py:220
  27.2 0.0 copy-done.1
  27.2 0.1 collective-permute-start.1
  27.3 0.2 collective-permute-done.3.refs_4_
  27.4 6.8 %collective-permute-done.4.refs_5_ = bf16[720,256]{1,0:T(8,128)(2,1)S(1)} collective-permute-done((bf16[720,256]{1,0:T(8,128)(2,1)S(1)}, bf16[720,256]{1,0:T(8,128)(2,1)S(1)}, u32[]{:S(2)}, u32[]{:S(2)}) %collective-permute-start.4) | collective-permute-done | bytes 368672 | tf_op jit(solution)/shard_map/ppermute | solution.py:220
  34.2 4.0 %collective-permute-done.5.refs_2_ = bf16[1440,256]{1,0:T(8,128)(2,1)} collective-permute-done((bf16[1440,256]{1,0:T(8,128)(2,1)S(1)}, bf16[1440,256]{1,0:T(8,128)(2,1)}, u32[]{:S(2)}, u32[]{:S(2)}) %collective-permute-start.5) | collective-permute-done | bytes 737312 | tf_op jit(solution)/shard_map/ppermute | solution.py:220
  38.2 4.6 %collective-permute-start.8 = (bf16[1440,256]{1,0:T(8,128)(2,1)}, bf16[1440,256]{1,0:T(8,128)(2,1)}, u32[]{:S(2)}, u32[]{:S(2)}) collective-permute-start(bf16[1440,256]{1,0:T(8,128)(2,1)} %collective-permute-done.5.refs_2_), channel_id=1, source_target_pairs={{0,4},{1,5},{4,8},{5,9},{8,12},{9,13},{6,2},{7,3},{10,6},{11,7},{1... | collective-permute-start | bytes 2211848 | tf_op jit(solution)/shard_map/ppermute | solution.py:220
  42.8 0.1 collective-permute-start.7
  43.0 0.6 collective-permute-start.6
  43.5 0.1 collective-permute-start.11
  43.6 0.0 collective-permute-done.1.refs_1_
  43.6 1.0 %collective-permute-done.7.refs_7_ = bf16[720,256]{1,0:T(8,128)(2,1)S(1)} collective-permute-done((bf16[720,256]{1,0:T(8,128)(2,1)S(1)}, bf16[720,256]{1,0:T(8,128)(2,1)S(1)}, u32[]{:S(2)}, u32[]{:S(2)}) %collective-permute-start.7) | collective-permute-done | bytes 368672 | tf_op jit(solution)/shard_map/ppermute | solution.py:220
  44.6 0.5 collective-permute-done.6.refs_6_
  45.1 0.0 copy-done.3
  45.1 0.0 copy-done.4
  45.1 0.0 copy-done.5
  45.1 0.0 copy-done.6
  45.1 0.2 copy-done.8
  45.3 0.7 copy-done.9
  46.1 11.9 %forward_layer.1 = (bf16[1440,256]{1,0:T(8,128)(2,1)}, bf16[8,144,256]{2,1,0:T(8,128)(2,1)}, bf16[8,144,256]{2,1,0:T(8,128)(2,1)}) custom-call(s32[7]{0:T(128)} %stack.23.meta, bf16[1440,256]{1,0:T(8,128)(2,1)} %bitcast.39, bf16[1440,256]{1,0:T(8,128)(2,1)} %collective-permute-done.1.refs_1_, bf16[720,256]{1,0:T(8,128)(2,1)} %copy-done.3, ...), custom_call_target="tpu_custom_call" | custom-call | flops 1 | tf_op jit(solution)/shard_map/forward_layer/pallas_call | solution.py:182
  57.9 0.0 copy-start.7
  58.0 0.0 collective-permute-done.8.refs_3_
  58.0 0.2 collective-permute-start.9
  58.2 1.2 %broadcast_select_fusion = bf16[1440,256]{1,0:T(8,128)(2,1)S(1)} fusion(bf16[1440,256]{1,0:T(8,128)(2,1)} %collective-permute-done.5.refs_2_, bf16[1440,256]{1,0:T(8,128)(2,1)} %collective-permute-done.8.refs_3_, pred[]{:T(512)S(6)} %eq.21), kind=kLoop, calls=%fused_computation.2 | loop fusion | flops 368640 | bytes 2211841 | tf_op jit(solution)/shard_map/jit(_where)/select_n | solution.py:240
  59.4 0.4 collective-permute-start.12
  59.8 0.4 collective-permute-done.9
  60.3 0.0 copy-done.7
  60.3 0.1 add_convert_fusion
  60.4 1.5 %collective-permute-start.10 = (bf16[4,144,256]{2,1,0:T(8,128)(2,1)S(1)}, bf16[4,144,256]{2,1,0:T(8,128)(2,1)S(1)}, u32[]{:S(2)}, u32[]{:S(2)}) collective-permute-start(bf16[4,144,256]{2,1,0:T(8,128)(2,1)S(1)} %dynamic-slice_bitcast_fusion), channel_id=1, source_target_pairs={{0,2},{1,3},{2,0},{3,1},{4,6},{5,7},{6,4},{7,5},{8,10},{9,11},{10,... | collective-permute-start | bytes 884744 | tf_op jit(solution)/shard_map/ppermute | solution.py:220
  62.0 0.0 collective-permute-done.11.refs_1_
  62.0 0.0 collective-permute-done.12.refs_4_
  62.0 0.9 %copy-done.12 = bf16[1440,256]{1,0:T(8,128)(2,1)} copy-done((bf16[1440,256]{1,0:T(8,128)(2,1)}, bf16[1440,256]{1,0:T(8,128)(2,1)S(1)}, u32[]{:S(2)}) %copy-start.12) | copy-done | bytes 737304
  62.8 9.1 %backward_layer.1 = bf16[1440,256]{1,0:T(8,128)(2,1)} custom-call(s32[7]{0:T(128)} %stack.23.meta, bf16[1440,256]{1,0:T(8,128)(2,1)} %bitcast.41, bf16[1440,256]{1,0:T(8,128)(2,1)} %collective-permute-done.11.refs_1_, bf16[1440,256]{1,0:T(8,128)(2,1)} %collective-permute-done.5.refs_2_, bf16[1440,256]{1,0:T(8,128)(2,1)} %collective-permute-done.8.refs_3_, ...), custom_call_target="tpu_custom_call" | custom-call | flops 5000000000 | bytes 50000000 | tf_op jit(solution)/shard_map/backward_layer/pallas_call | solution.py:182
  71.9 0.0 collective-permute-done.10
  71.9 0.1 fusion
  72.0 1.6 %collective-permute-start.13 = (bf16[2,144,256]{2,1,0:T(8,128)(2,1)S(1)}, bf16[2,144,256]{2,1,0:T(8,128)(2,1)S(1)}, u32[]{:S(2)}, u32[]{:S(2)}) collective-permute-start(bf16[2,144,256]{2,1,0:T(8,128)(2,1)S(1)} %dynamic-slice_bitcast_fusion.1), channel_id=1, source_target_pairs={{0,4},{1,5},{2,6},{3,7},{4,0},{5,1},{6,2},{7,3},{8,12},{9,13},{10,... | collective-permute-start | bytes 442376 | tf_op jit(solution)/shard_map/ppermute | solution.py:220
  73.7 4.2 %collective-permute-done.13 = bf16[2,144,256]{2,1,0:T(8,128)(2,1)S(1)} collective-permute-done((bf16[2,144,256]{2,1,0:T(8,128)(2,1)S(1)}, bf16[2,144,256]{2,1,0:T(8,128)(2,1)S(1)}, u32[]{:S(2)}, u32[]{:S(2)}) %collective-permute-start.13) | collective-permute-done | bytes 147488 | tf_op jit(solution)/shard_map/ppermute | solution.py:220
  78.0 2.6 %collective-permute-start.14 = (bf16[1,144,256]{2,1,0:T(8,128)(2,1)S(1)}, bf16[1,144,256]{2,1,0:T(8,128)(2,1)S(1)}, u32[]{:S(2)}, u32[]{:S(2)}) collective-permute-start(bf16[1,144,256]{2,1,0:T(8,128)(2,1)S(1)} %constant_dynamic-slice_fusion), channel_id=1, source_target_pairs={{0,8},{1,9},{2,10},{3,11},{4,12},{5,13},{6,14},{7,15},{8,0},{9,1},... | collective-permute-start | bytes 221192 | tf_op jit(solution)/shard_map/ppermute | solution.py:220
  80.6 3.0 %collective-permute-done.14 = bf16[1,144,256]{2,1,0:T(8,128)(2,1)S(1)} collective-permute-done((bf16[1,144,256]{2,1,0:T(8,128)(2,1)S(1)}, bf16[1,144,256]{2,1,0:T(8,128)(2,1)S(1)}, u32[]{:S(2)}, u32[]{:S(2)}) %collective-permute-start.14) | collective-permute-done | bytes 73760 | tf_op jit(solution)/shard_map/ppermute | solution.py:220
  83.6 0.7 multiply_bitcast_fusion
  (19 shorter events, 0.2 us)
Async XLA Ops:
  0.6 5.0 %copy-start.10 = (s32[16,5,7]{0,2,1:T(8,128)S(1)}, s32[16,5,7]{0,2,1:T(8,128)}, u32[]{:S(2)}) copy-start(s32[16,5,7]{0,2,1:T(8,128)} %param.14) | copy-start | bytes 6724
  2.7 3.9 %copy-start.11 = (f32[16,5,7]{0,2,1:T(8,128)S(1)}, f32[16,5,7]{0,2,1:T(8,128)}, u32[]{:S(2)}) copy-start(f32[16,5,7]{0,2,1:T(8,128)} %param.15) | copy-start | bytes 6724
  2.7 4.7 %slice-start = ((bf16[1,1440,256]{2,1,0:T(8,128)(2,1)}), bf16[1,1432,256]{2,1,0:T(8,128)(2,1)S(1)}, s32[]{:S(2)}) async-start(bf16[1,1440,256]{2,1,0:T(8,128)(2,1)} %param.9), calls=%async_computation | async-start | bytes 1466368 | tf_op jit(solution)/shard_map/jit(_roll_static)/slice | solution.py:243
  2.7 12.6 %collective-permute-start = (bf16[720,256]{1,0:T(8,128)(2,1)}, bf16[720,256]{1,0:T(8,128)(2,1)S(1)}, u32[]{:S(2)}, u32[]{:S(2)}) collective-permute-start(bf16[720,256]{1,0:T(8,128)(2,1)} %get-tuple-element.40), channel_id=1, source_target_pairs={{0,2},{1,3},{2,0},{3,1},{4,6},{5,7},{6,4},{7,5},{8,10},{9,11},{10,... | collective-permute-start | bytes 1105928 | tf_op jit(solution)/shard_map/ppermute | solution.py:220
  5.6 17.5 %collective-permute-start.2 = (bf16[720,256]{1,0:T(8,128)(2,1)}, bf16[720,256]{1,0:T(8,128)(2,1)S(1)}, u32[]{:S(2)}, u32[]{:S(2)}) collective-permute-start(bf16[720,256]{1,0:T(8,128)(2,1)} %get-tuple-element.39), channel_id=1, source_target_pairs={{0,2},{1,3},{2,0},{3,1},{4,6},{5,7},{6,4},{7,5},{8,10},{9,11},{10,... | collective-permute-start | bytes 1105928 | tf_op jit(solution)/shard_map/ppermute | solution.py:220
  5.7 2.0 %slice-start.1 = ((bf16[1,1440,256]{2,1,0:T(8,128)(2,1)}), bf16[1,8,256]{2,1,0:T(8,128)(2,1)S(1)}, s32[]{:S(2)}) async-start(bf16[1,1440,256]{2,1,0:T(8,128)(2,1)} %param.9), calls=%async_computation.1 | async-start | bytes 8192 | tf_op jit(solution)/shard_map/jit(_roll_static)/slice | solution.py:243
  5.7 2.1 %copy-start = (bf16[2304,256]{1,0:T(8,128)(2,1)S(1)}, bf16[2304,256]{1,0:T(8,128)(2,1)}, u32[]{:S(2)}) copy-start(bf16[2304,256]{1,0:T(8,128)(2,1)} %refs_9_.1) | copy-start | bytes 3538948
  9.4 5.9 %copy-start.2 = (bf16[1,1440,256]{2,1,0:T(8,128)(2,1)S(1)}, bf16[1,1440,256]{2,1,0:T(8,128)(2,1)}, u32[]{:S(2)}) copy-start(bf16[1,1440,256]{2,1,0:T(8,128)(2,1)} %param.9) | copy-start | bytes 2211844
  9.4 17.8 %copy-start.1 = (bf16[1,1440,256]{2,1,0:T(8,128)(2,1)S(1)}, bf16[1,1440,256]{2,1,0:T(8,128)(2,1)}, u32[]{:S(2)}) copy-start(bf16[1,1440,256]{2,1,0:T(8,128)(2,1)} %param.8) | copy-start | bytes 2211844
  15.2 29.9 %copy-start.3 = (bf16[720,256]{1,0:T(8,128)(2,1)}, bf16[720,256]{1,0:T(8,128)(2,1)S(1)}, u32[]{:S(2)}) copy-start(bf16[720,256]{1,0:T(8,128)(2,1)S(1)} %collective-permute-done.refs_2_) | copy-start | bytes 1105924
  15.2 23.0 %collective-permute-start.5 = (bf16[1440,256]{1,0:T(8,128)(2,1)S(1)}, bf16[1440,256]{1,0:T(8,128)(2,1)}, u32[]{:S(2)}, u32[]{:S(2)}) collective-permute-start(bf16[1440,256]{1,0:T(8,128)(2,1)S(1)} %bitcast.42), channel_id=1, source_target_pairs={{0,2},{1,3},{2,0},{3,1},{4,6},{5,7},{6,4},{7,5},{8,10},{9,11},{10,... | collective-permute-start | bytes 2211848 | tf_op jit(solution)/shard_map/ppermute | solution.py:220
  17.3 10.2 %collective-permute-start.3 = (bf16[720,256]{1,0:T(8,128)(2,1)S(1)}, bf16[720,256]{1,0:T(8,128)(2,1)S(1)}, u32[]{:S(2)}, u32[]{:S(2)}) collective-permute-start(bf16[720,256]{1,0:T(8,128)(2,1)S(1)} %collective-permute-done.refs_2_), channel_id=1, source_target_pairs={{0,4},{1,5},{4,8},{5,9},{8,12},{9,13},{6,2},{7,3},{10,6},{11,7},{1... | collective-permute-start | bytes 1105928 | tf_op jit(solution)/shard_map/ppermute | solution.py:220
  23.1 22.0 %copy-start.4 = (bf16[720,256]{1,0:T(8,128)(2,1)}, bf16[720,256]{1,0:T(8,128)(2,1)S(1)}, u32[]{:S(2)}) copy-start(bf16[720,256]{1,0:T(8,128)(2,1)S(1)} %collective-permute-done.2.refs_3_) | copy-start | bytes 1105924
  23.1 11.1 %collective-permute-start.4 = (bf16[720,256]{1,0:T(8,128)(2,1)S(1)}, bf16[720,256]{1,0:T(8,128)(2,1)S(1)}, u32[]{:S(2)}, u32[]{:S(2)}) collective-permute-start(bf16[720,256]{1,0:T(8,128)(2,1)S(1)} %collective-permute-done.2.refs_3_), channel_id=1, source_target_pairs={{0,4},{1,5},{4,8},{5,9},{8,12},{9,13},{6,2},{7,3},{10,6},{11,7},{1... | collective-permute-start | bytes 1105928 | tf_op jit(solution)/shard_map/ppermute | solution.py:220
  27.2 16.4 %collective-permute-start.1 = (bf16[1440,256]{1,0:T(8,128)(2,1)S(1)}, bf16[1440,256]{1,0:T(8,128)(2,1)}, u32[]{:S(2)}, u32[]{:S(2)}) collective-permute-start(bf16[1440,256]{1,0:T(8,128)(2,1)S(1)} %bitcast.40), channel_id=1, source_target_pairs={{0,1},{1,0},{2,3},{3,2},{4,5},{5,4},{6,7},{7,6},{8,9},{9,8},{10,11... | collective-permute-start | bytes 2211848 | tf_op jit(solution)/shard_map/ppermute | solution.py:220
  27.4 17.7 %copy-start.5 = (bf16[720,256]{1,0:T(8,128)(2,1)}, bf16[720,256]{1,0:T(8,128)(2,1)S(1)}, u32[]{:S(2)}) copy-start(bf16[720,256]{1,0:T(8,128)(2,1)S(1)} %collective-permute-done.3.refs_4_) | copy-start | bytes 1105924
  34.2 10.9 %copy-start.6 = (bf16[720,256]{1,0:T(8,128)(2,1)}, bf16[720,256]{1,0:T(8,128)(2,1)S(1)}, u32[]{:S(2)}) copy-start(bf16[720,256]{1,0:T(8,128)(2,1)S(1)} %collective-permute-done.4.refs_5_) | copy-start | bytes 1105924
  38.2 19.8 %collective-permute-start.8 = (bf16[1440,256]{1,0:T(8,128)(2,1)}, bf16[1440,256]{1,0:T(8,128)(2,1)}, u32[]{:S(2)}, u32[]{:S(2)}) collective-permute-start(bf16[1440,256]{1,0:T(8,128)(2,1)} %collective-permute-done.5.refs_2_), channel_id=1, source_target_pairs={{0,4},{1,5},{4,8},{5,9},{8,12},{9,13},{6,2},{7,3},{10,6},{11,7},{1... | collective-permute-start | bytes 2211848 | tf_op jit(solution)/shard_map/ppermute | solution.py:220
  42.8 1.8 %collective-permute-start.7 = (bf16[720,256]{1,0:T(8,128)(2,1)S(1)}, bf16[720,256]{1,0:T(8,128)(2,1)S(1)}, u32[]{:S(2)}, u32[]{:S(2)}) collective-permute-start(bf16[720,256]{1,0:T(8,128)(2,1)S(1)} %broadcast_select_fusion.1), channel_id=1, source_target_pairs={{0,1},{1,0},{2,3},{3,2},{4,5},{5,4},{6,7},{7,6},{8,9},{9,8},{10,11... | collective-permute-start | bytes 1105928 | tf_op jit(solution)/shard_map/ppermute | solution.py:220
  43.0 2.2 %collective-permute-start.6 = (bf16[720,256]{1,0:T(8,128)(2,1)S(1)}, bf16[720,256]{1,0:T(8,128)(2,1)S(1)}, u32[]{:S(2)}, u32[]{:S(2)}) collective-permute-start(bf16[720,256]{1,0:T(8,128)(2,1)S(1)} %broadcast_select_fusion.2), channel_id=1, source_target_pairs={{0,1},{1,0},{2,3},{3,2},{4,5},{5,4},{6,7},{7,6},{8,9},{9,8},{10,11... | collective-permute-start | bytes 1105928 | tf_op jit(solution)/shard_map/ppermute | solution.py:220
  43.5 18.5 %collective-permute-start.11 = (bf16[1440,256]{1,0:T(8,128)(2,1)S(1)}, bf16[1440,256]{1,0:T(8,128)(2,1)}, u32[]{:S(2)}, u32[]{:S(2)}) collective-permute-start(bf16[1440,256]{1,0:T(8,128)(2,1)S(1)} %bitcast.43), channel_id=1, source_target_pairs={{0,1},{1,0},{2,3},{3,2},{4,5},{5,4},{6,7},{7,6},{8,9},{9,8},{10,11... | collective-permute-start | bytes 2211848 | tf_op jit(solution)/shard_map/ppermute | solution.py:220
  44.6 0.8 copy-start.8
  45.3 0.7 copy-start.9
  57.9 2.3 %copy-start.7 = (bf16[8,144,256]{2,1,0:T(8,128)(2,1)S(1)}, bf16[8,144,256]{2,1,0:T(8,128)(2,1)}, u32[]{:S(2)}) copy-start(bf16[8,144,256]{2,1,0:T(8,128)(2,1)} %get-tuple-element.31) | copy-start | bytes 1769476
  58.0 2.3 %collective-permute-start.9 = (bf16[8,144,256]{2,1,0:T(8,128)(2,1)}, bf16[8,144,256]{2,1,0:T(8,128)(2,1)S(1)}, u32[]{:S(2)}, u32[]{:S(2)}) collective-permute-start(bf16[8,144,256]{2,1,0:T(8,128)(2,1)} %get-tuple-element.33), channel_id=1, source_target_pairs={{0,1},{1,0},{2,3},{3,2},{4,5},{5,4},{6,7},{7,6},{8,9},{9,8},{10,11... | collective-permute-start | bytes 1769480 | tf_op jit(solution)/shard_map/ppermute | solution.py:220
  59.4 2.6 %collective-permute-start.12 = (bf16[1440,256]{1,0:T(8,128)(2,1)S(1)}, bf16[1440,256]{1,0:T(8,128)(2,1)S(1)}, u32[]{:S(2)}, u32[]{:S(2)}) collective-permute-start(bf16[1440,256]{1,0:T(8,128)(2,1)S(1)} %broadcast_select_fusion), channel_id=1, source_target_pairs={{0,1},{1,0},{2,3},{3,2},{4,5},{5,4},{6,7},{7,6},{8,9},{9,8},{10,11... | collective-permute-start | bytes 2211848 | tf_op jit(solution)/shard_map/ppermute | solution.py:220
  60.4 11.5 %collective-permute-start.10 = (bf16[4,144,256]{2,1,0:T(8,128)(2,1)S(1)}, bf16[4,144,256]{2,1,0:T(8,128)(2,1)S(1)}, u32[]{:S(2)}, u32[]{:S(2)}) collective-permute-start(bf16[4,144,256]{2,1,0:T(8,128)(2,1)S(1)} %dynamic-slice_bitcast_fusion), channel_id=1, source_target_pairs={{0,2},{1,3},{2,0},{3,1},{4,6},{5,7},{6,4},{7,5},{8,10},{9,11},{10,... | collective-permute-start | bytes 884744 | tf_op jit(solution)/shard_map/ppermute | solution.py:220
  62.0 0.9 %copy-start.12 = (bf16[1440,256]{1,0:T(8,128)(2,1)}, bf16[1440,256]{1,0:T(8,128)(2,1)S(1)}, u32[]{:S(2)}) copy-start(bf16[1440,256]{1,0:T(8,128)(2,1)S(1)} %collective-permute-done.12.refs_4_) | copy-start | bytes 2211844
  72.0 5.9 %collective-permute-start.13 = (bf16[2,144,256]{2,1,0:T(8,128)(2,1)S(1)}, bf16[2,144,256]{2,1,0:T(8,128)(2,1)S(1)}, u32[]{:S(2)}, u32[]{:S(2)}) collective-permute-start(bf16[2,144,256]{2,1,0:T(8,128)(2,1)S(1)} %dynamic-slice_bitcast_fusion.1), channel_id=1, source_target_pairs={{0,4},{1,5},{2,6},{3,7},{4,0},{5,1},{6,2},{7,3},{8,12},{9,13},{10,... | collective-permute-start | bytes 442376 | tf_op jit(solution)/shard_map/ppermute | solution.py:220
  78.0 5.6 %collective-permute-start.14 = (bf16[1,144,256]{2,1,0:T(8,128)(2,1)S(1)}, bf16[1,144,256]{2,1,0:T(8,128)(2,1)S(1)}, u32[]{:S(2)}, u32[]{:S(2)}) collective-permute-start(bf16[1,144,256]{2,1,0:T(8,128)(2,1)S(1)} %constant_dynamic-slice_fusion), channel_id=1, source_target_pairs={{0,8},{1,9},{2,10},{3,11},{4,12},{5,13},{6,14},{7,15},{8,0},{9,1},... | collective-permute-start | bytes 221192 | tf_op jit(solution)/shard_map/ppermute | solution.py:220

commit v3 on v2

--- a/solution.py
+++ b/solution.py
@@ -24,7 +24,7 @@
 LATE = 4
 HOLD = True
 CUTS_F = (720,)
-CUTS_B = ()
+CUTS_B = (960,)
 SHIFT = 8
 
 
@@ -256,7 +256,7 @@
     signal_farther = [sent(piece, onward) for piece in signal_far]
     cotangent_farther = [sent(piece, onward) for piece in cotangent_far]
     if HOLD:
-        signal_farther, _ = lax.optimization_barrier((signal_farther, cotangent_far))
+        signal_farther, _ = lax.optimization_barrier((signal_farther, cotangent_far[0]))
     signal_extra = swapped(signal_far, signal_farther)
     signal_rows = [[signal], [signal_beside], signal_far, signal_farther, signal_extra]
     cotangent_rows = [[cotangent], [cotangent_beside], cotangent_far, cotangent_farther, None]

time: 84.6 us -> 83.3 us (0.985)
  waiting for transfers between devices: 24.7 us -> 18.7 us
  starting transfers between devices: 24.4 us -> 27.4 us
  other arithmetic: 3.21 us -> 4.1 us
    ppermute x15 -> x18, waiting for transfers between devices: 24.7 us -> 18.7 us  [sent(): return lax.ppermute(array, 'lat', pairs)]
    ppermute x15 -> x18, starting transfers between devices: 24.4 us -> 27.4 us  [sent(): return lax.ppermute(array, 'lat', pairs)]
    select_n x3 -> x4, other arithmetic: 1.28 us -> 2.15 us  [swapped(): jnp.where(side == core, one, other)]
    unnamed x30 -> x34, local copies, waits for them, and re-layouts: 2.47 us -> 2.85 us
    slice x1 -> x3, local copies, waits for them, and re-layouts: 2.01 us -> 2.06 us  [split(): return [row[low:high] for low, high in zip(edges, edges[1:])]]
  transfers between devices with their start and end apart: 15 -> 18, of which waited for: 10 -> 7; matrix products, arithmetic and copies ran while one was open for 8% -> 9% of each run, Pallas kernels for 27% -> 28%
where the time goes in v3:
time: 83.3 us; the launch traced here: 82.9 us
  starting transfers between devices  27.4 us (33%)
  Pallas kernels  23 us (28%)
  waiting for transfers between devices  18.7 us (22%)
  local copies, waits for them, and re-layouts  8.65 us (10%)
  other arithmetic  4.1 us (5%)
  between operations  1 us (1%)
    ppermute x18, starting transfers between devices, sent(): return lax.ppermute(array, 'lat', pairs)  27.4 us
    pallas_call x2, Pallas kernels, layer(): pl.pallas_call(functools.partial(layer_kernel, counts), out_shape=outs, i...  21.1 us
    ppermute x18, waiting for transfers between devices, sent(): return lax.ppermute(array, 'lat', pairs)  18.7 us
    unnamed x34, local copies, waits for them, and re-layouts  2.85 us
    select_n x4, other arithmetic, swapped(): jnp.where(side == core, one, other)  2.15 us
    slice x3, local copies, waits for them, and re-layouts, split(): return [row[low:high] for low, high in zip(edges, edges[1:])]  2.06 us
    pallas_call x1, Pallas kernels, bands(): pl.pallas_call(bands_kernel, out_shape=[jax.ShapeDtypeStruct(BAND, jnp.bf...  1.92 us
  transfers between devices with their start and end apart: 18, of which 7 were waited for; matrix products, arithmetic and copies ran while one was open for 9% of the time, Pallas kernels for 28%

profile of v3, /device:TPU:0, one launch (start us, length us, event | category | flops | bytes accessed | tf_op | source)
XLA Modules:
  0.0 82.9 jit_solution(5703170656421786070)
XLA Ops:
  0.6 0.0 copy-start.12
  0.6 2.0 %slice_bitcast_fusion = (bf16[720,256]{1,0:T(8,128)(2,1)}, bf16[720,256]{1,0:T(8,128)(2,1)}) fusion(bf16[1,1440,256]{2,1,0:T(8,128)(2,1)} %param.8), kind=kLoop, calls=%fused_computation.5 | loop fusion | bytes 1474560 | tf_op jit(solution)/shard_map/slice | solution.py:237
  2.7 2.9 %collective-permute-start = (bf16[720,256]{1,0:T(8,128)(2,1)}, bf16[720,256]{1,0:T(8,128)(2,1)S(1)}, u32[]{:S(2)}, u32[]{:S(2)}) collective-permute-start(bf16[720,256]{1,0:T(8,128)(2,1)} %get-tuple-element.42), channel_id=1, source_target_pairs={{0,2},{1,3},{2,0},{3,1},{4,6},{5,7},{6,4},{7,5},{8,10},{9,11},{10,... | collective-permute-start | bytes 1105928 | tf_op jit(solution)/shard_map/ppermute | solution.py:220
  5.6 0.1 collective-permute-start.2
  5.7 0.0 copy-done.12
  5.7 0.1 copy.17
  5.8 0.7 reshape.43.basis
  6.5 0.1 copy.18
  6.7 0.7 reshape.44.quad
  7.4 0.3 copy.20
  7.7 0.1 copy.21
  7.8 1.6 %copy.16 = bf16[9,256,256]{1,2,0:T(8,128)(2,1)} copy(bf16[9,256,256]{2,1,0:T(8,128)(2,1)S(1)} %bitcast.37) | data formatting | bytes 2359296 | tf_op jit(solution)/shard_map/reshape | solution.py:244
  9.4 0.6 stack.23.meta
  10.0 1.9 %bands.1 = (bf16[288,240]{1,0:T(8,128)(2,1)}, bf16[288,240]{1,0:T(8,128)(2,1)}) custom-call(s32[7]{0:T(128)} %stack.23.meta, s32[16]{0:T(128)} %first.1, s32[16]{0:T(128)} %last.1, s32[16]{0:T(128)} %reach.1, s32[560]{0:T(1024)} %reshape.43.basis, f32[560]{0:T(1024)} %reshape.44.quad), custom_call_target="tpu_custom_call" | custom-call | tf_op jit(solution)/shard_map/bands/pallas_call | solution.py:71
  11.9 1.0 %maximum_bitcast_fusion.refs_10_ = bf16[256,1440]{1,0:T(8,128)(2,1)} fusion(bf16[8,256]{0,1:T(8,128)(2,1)S(1)} %bitcast.50, bf16[1432,256]{0,1:T(8,128)(2,1)S(1)} %bitcast.38), kind=kLoop, calls=%fused_computation.1 | loop fusion | flops 1474560 | bytes 1474560 | tf_op jit(solution)/shard_map/transpose | solution.py:243
  12.9 2.3 %collective-permute-done.refs_2_ = bf16[720,256]{1,0:T(8,128)(2,1)S(1)} collective-permute-done((bf16[720,256]{1,0:T(8,128)(2,1)}, bf16[720,256]{1,0:T(8,128)(2,1)S(1)}, u32[]{:S(2)}, u32[]{:S(2)}) %collective-permute-start) | collective-permute-done | bytes 368672 | tf_op jit(solution)/shard_map/ppermute | solution.py:220
  15.3 2.1 %collective-permute-start.5 = (bf16[960,256]{1,0:T(8,128)(2,1)S(1)}, bf16[960,256]{1,0:T(8,128)(2,1)}, u32[]{:S(2)}, u32[]{:S(2)}) collective-permute-start(bf16[960,256]{1,0:T(8,128)(2,1)S(1)} %slice.40), channel_id=1, source_target_pairs={{0,2},{1,3},{2,0},{3,1},{4,6},{5,7},{6,4},{7,5},{8,10},{9,11},{10,... | collective-permute-start | bytes 1474568 | tf_op jit(solution)/shard_map/ppermute | solution.py:220
  17.4 3.5 %collective-permute-start.3 = (bf16[720,256]{1,0:T(8,128)(2,1)S(1)}, bf16[720,256]{1,0:T(8,128)(2,1)S(1)}, u32[]{:S(2)}, u32[]{:S(2)}) collective-permute-start(bf16[720,256]{1,0:T(8,128)(2,1)S(1)} %collective-permute-done.refs_2_), channel_id=1, source_target_pairs={{0,4},{1,5},{4,8},{5,9},{8,12},{9,13},{6,2},{7,3},{10,6},{11,7},{1... | collective-permute-start | bytes 1105928 | tf_op jit(solution)/shard_map/ppermute | solution.py:220
  20.9 2.2 %collective-permute-done.2.refs_3_ = bf16[720,256]{1,0:T(8,128)(2,1)S(1)} collective-permute-done((bf16[720,256]{1,0:T(8,128)(2,1)}, bf16[720,256]{1,0:T(8,128)(2,1)S(1)}, u32[]{:S(2)}, u32[]{:S(2)}) %collective-permute-start.2) | collective-permute-done | bytes 368672 | tf_op jit(solution)/shard_map/ppermute | solution.py:220
  23.1 4.1 %collective-permute-start.4 = (bf16[720,256]{1,0:T(8,128)(2,1)S(1)}, bf16[720,256]{1,0:T(8,128)(2,1)S(1)}, u32[]{:S(2)}, u32[]{:S(2)}) collective-permute-start(bf16[720,256]{1,0:T(8,128)(2,1)S(1)} %collective-permute-done.2.refs_3_), channel_id=1, source_target_pairs={{0,4},{1,5},{4,8},{5,9},{8,12},{9,13},{6,2},{7,3},{10,6},{11,7},{1... | collective-permute-start | bytes 1105928 | tf_op jit(solution)/shard_map/ppermute | solution.py:220
  27.2 0.1 collective-permute-start.1
  27.3 0.1 collective-permute-start.9
  27.4 0.2 collective-permute-done.3.refs_4_
  27.6 6.7 %collective-permute-done.4.refs_5_ = bf16[720,256]{1,0:T(8,128)(2,1)S(1)} collective-permute-done((bf16[720,256]{1,0:T(8,128)(2,1)S(1)}, bf16[720,256]{1,0:T(8,128)(2,1)S(1)}, u32[]{:S(2)}, u32[]{:S(2)}) %collective-permute-start.4) | collective-permute-done | bytes 368672 | tf_op jit(solution)/shard_map/ppermute | solution.py:220
  34.3 0.0 collective-permute-done.5.refs_2_
  34.3 0.1 collective-permute-start.7
  34.4 4.4 %collective-permute-start.8 = (bf16[960,256]{1,0:T(8,128)(2,1)}, bf16[960,256]{1,0:T(8,128)(2,1)S(1)}, u32[]{:S(2)}, u32[]{:S(2)}) collective-permute-start(bf16[960,256]{1,0:T(8,128)(2,1)} %collective-permute-done.5.refs_2_), channel_id=1, source_target_pairs={{0,4},{1,5},{4,8},{5,9},{8,12},{9,13},{6,2},{7,3},{10,6},{11,7},{1... | collective-permute-start | bytes 1474568 | tf_op jit(solution)/shard_map/ppermute | solution.py:220
  38.9 0.3 collective-permute-start.6
  39.2 0.0 collective-permute-done.9.refs_3_
  39.2 3.5 %collective-permute-start.10 = (bf16[480,256]{1,0:T(8,128)(2,1)}, bf16[480,256]{1,0:T(8,128)(2,1)S(1)}, u32[]{:S(2)}, u32[]{:S(2)}) collective-permute-start(bf16[480,256]{1,0:T(8,128)(2,1)} %collective-permute-done.9.refs_3_), channel_id=1, source_target_pairs={{0,4},{1,5},{4,8},{5,9},{8,12},{9,13},{6,2},{7,3},{10,6},{11,7},{1... | collective-permute-start | bytes 737288 | tf_op jit(solution)/shard_map/ppermute | solution.py:220
  42.7 0.0 collective-permute-done.1.refs_1_
  42.7 0.0 collective-permute-done.7.refs_7_
  42.7 0.0 collective-permute-done.6.refs_6_
  42.7 0.0 copy-done.5
  42.7 0.0 copy-done.6
  42.7 0.7 copy-done.9
  43.4 0.7 copy-done.10
  44.2 11.9 %forward_layer.1 = (bf16[1440,256]{1,0:T(8,128)(2,1)}, bf16[8,144,256]{2,1,0:T(8,128)(2,1)}, bf16[8,144,256]{2,1,0:T(8,128)(2,1)}) custom-call(s32[7]{0:T(128)} %stack.23.meta, bf16[1440,256]{1,0:T(8,128)(2,1)} %bitcast.39, bf16[1440,256]{1,0:T(8,128)(2,1)} %collective-permute-done.1.refs_1_, bf16[720,256]{1,0:T(8,128)(2,1)} %copy-done.3, ...), custom_call_target="tpu_custom_call" | custom-call | flops 1 | tf_op jit(solution)/shard_map/forward_layer/pallas_call | solution.py:182
  56.0 0.0 copy-start.7
  56.1 0.0 collective-permute-done.10.refs_5_
  56.1 0.0 collective-permute-done.8.refs_4_
  56.1 0.0 copy-start.8
  56.1 0.1 collective-permute-start.11
  56.2 0.5 collective-permute-start.13
  56.7 1.1 %broadcast_select_fusion = bf16[960,256]{1,0:T(8,128)(2,1)S(1)} fusion(bf16[960,256]{1,0:T(8,128)(2,1)} %collective-permute-done.5.refs_2_, bf16[960,256]{1,0:T(8,128)(2,1)S(1)} %collective-permute-done.8.refs_4_, pred[]{:T(512)S(6)} %eq.22), kind=kLoop, calls=%fused_computation.4 | loop fusion | flops 245760 | bytes 1474561 | tf_op jit(solution)/shard_map/jit(_where)/select_n | solution.py:240
  57.8 0.1 collective-permute-start.14
  57.8 1.0 %broadcast_select_fusion.3 = bf16[480,256]{1,0:T(8,128)(2,1)S(1)} fusion(bf16[480,256]{1,0:T(8,128)(2,1)} %collective-permute-done.9.refs_3_, bf16[480,256]{1,0:T(8,128)(2,1)S(1)} %collective-permute-done.10.refs_5_, pred[]{:T(512)S(6)} %eq.22), kind=kLoop, calls=%fused_computation.12 | loop fusion | flops 122880 | bytes 737281 | tf_op jit(solution)/shard_map/jit(_where)/select_n | solution.py:240
  58.8 0.1 collective-permute-start.15
  58.9 0.0 collective-permute-done.11
  58.9 0.0 copy-done.7
  58.9 0.1 add_convert_fusion
  59.1 0.9 %collective-permute-start.12 = (bf16[4,144,256]{2,1,0:T(8,128)(2,1)S(1)}, bf16[4,144,256]{2,1,0:T(8,128)(2,1)S(1)}, u32[]{:S(2)}, u32[]{:S(2)}) collective-permute-start(bf16[4,144,256]{2,1,0:T(8,128)(2,1)S(1)} %dynamic-slice_bitcast_fusion), channel_id=1, source_target_pairs={{0,2},{1,3},{2,0},{3,1},{4,6},{5,7},{6,4},{7,5},{8,10},{9,11},{10,... | collective-permute-start | bytes 884744 | tf_op jit(solution)/shard_map/ppermute | solution.py:220
  60.1 0.0 collective-permute-done.13.refs_1_
  60.1 0.3 collective-permute-done.15.refs_7_
  60.4 0.0 collective-permute-done.14.refs_6_
  60.4 0.7 copy-done.14
  61.1 9.3 %backward_layer.1 = bf16[1440,256]{1,0:T(8,128)(2,1)} custom-call(s32[7]{0:T(128)} %stack.23.meta, bf16[1440,256]{1,0:T(8,128)(2,1)} %bitcast.41, bf16[1440,256]{1,0:T(8,128)(2,1)} %collective-permute-done.13.refs_1_, bf16[960,256]{1,0:T(8,128)(2,1)} %collective-permute-done.5.refs_2_, bf16[480,256]{1,0:T(8,128)(2,1)} %collective-permute-done.9.refs_3_, ...), custom_call_target="tpu_custom_call" | custom-call | flops 5000000000 | bytes 50000000 | tf_op jit(solution)/shard_map/backward_layer/pallas_call | solution.py:182
  70.4 0.0 collective-permute-done.12
  70.4 0.1 fusion
  70.5 1.8 %collective-permute-start.16 = (bf16[2,144,256]{2,1,0:T(8,128)(2,1)S(1)}, bf16[2,144,256]{2,1,0:T(8,128)(2,1)S(1)}, u32[]{:S(2)}, u32[]{:S(2)}) collective-permute-start(bf16[2,144,256]{2,1,0:T(8,128)(2,1)S(1)} %dynamic-slice_bitcast_fusion.1), channel_id=1, source_target_pairs={{0,4},{1,5},{2,6},{3,7},{4,0},{5,1},{6,2},{7,3},{8,12},{9,13},{10,... | collective-permute-start | bytes 442376 | tf_op jit(solution)/shard_map/ppermute | solution.py:220
  72.4 4.2 %collective-permute-done.16 = bf16[2,144,256]{2,1,0:T(8,128)(2,1)S(1)} collective-permute-done((bf16[2,144,256]{2,1,0:T(8,128)(2,1)S(1)}, bf16[2,144,256]{2,1,0:T(8,128)(2,1)S(1)}, u32[]{:S(2)}, u32[]{:S(2)}) %collective-permute-start.16) | collective-permute-done | bytes 147488 | tf_op jit(solution)/shard_map/ppermute | solution.py:220
  76.6 2.8 %collective-permute-start.17 = (bf16[1,144,256]{2,1,0:T(8,128)(2,1)S(1)}, bf16[1,144,256]{2,1,0:T(8,128)(2,1)S(1)}, u32[]{:S(2)}, u32[]{:S(2)}) collective-permute-start(bf16[1,144,256]{2,1,0:T(8,128)(2,1)S(1)} %constant_dynamic-slice_fusion), channel_id=1, source_target_pairs={{0,8},{1,9},{2,10},{3,11},{4,12},{5,13},{6,14},{7,15},{8,0},{9,1},... | collective-permute-start | bytes 221192 | tf_op jit(solution)/shard_map/ppermute | solution.py:220
  79.4 2.8 %collective-permute-done.17 = bf16[1,144,256]{2,1,0:T(8,128)(2,1)S(1)} collective-permute-done((bf16[1,144,256]{2,1,0:T(8,128)(2,1)S(1)}, bf16[1,144,256]{2,1,0:T(8,128)(2,1)S(1)}, u32[]{:S(2)}, u32[]{:S(2)}) %collective-permute-start.17) | collective-permute-done | bytes 73760 | tf_op jit(solution)/shard_map/ppermute | solution.py:220
  82.2 0.7 multiply_bitcast_fusion
  (32 shorter events, 0.3 us)
Async XLA Ops:
  0.6 5.0 %copy-start.12 = (s32[16,5,7]{0,2,1:T(8,128)S(1)}, s32[16,5,7]{0,2,1:T(8,128)}, u32[]{:S(2)}) copy-start(s32[16,5,7]{0,2,1:T(8,128)} %param.14) | copy-start | bytes 6724
  2.7 3.9 %copy-start.13 = (f32[16,5,7]{0,2,1:T(8,128)S(1)}, f32[16,5,7]{0,2,1:T(8,128)}, u32[]{:S(2)}) copy-start(f32[16,5,7]{0,2,1:T(8,128)} %param.15) | copy-start | bytes 6724
  2.7 4.7 %slice-start = ((bf16[1,1440,256]{2,1,0:T(8,128)(2,1)}), bf16[1,1432,256]{2,1,0:T(8,128)(2,1)S(1)}, s32[]{:S(2)}) async-start(bf16[1,1440,256]{2,1,0:T(8,128)(2,1)} %param.9), calls=%async_computation | async-start | bytes 1466368 | tf_op jit(solution)/shard_map/jit(_roll_static)/slice | solution.py:243
  2.7 12.6 %collective-permute-start = (bf16[720,256]{1,0:T(8,128)(2,1)}, bf16[720,256]{1,0:T(8,128)(2,1)S(1)}, u32[]{:S(2)}, u32[]{:S(2)}) collective-permute-start(bf16[720,256]{1,0:T(8,128)(2,1)} %get-tuple-element.42), channel_id=1, source_target_pairs={{0,2},{1,3},{2,0},{3,1},{4,6},{5,7},{6,4},{7,5},{8,10},{9,11},{10,... | collective-permute-start | bytes 1105928 | tf_op jit(solution)/shard_map/ppermute | solution.py:220
  5.6 17.5 %collective-permute-start.2 = (bf16[720,256]{1,0:T(8,128)(2,1)}, bf16[720,256]{1,0:T(8,128)(2,1)S(1)}, u32[]{:S(2)}, u32[]{:S(2)}) collective-permute-start(bf16[720,256]{1,0:T(8,128)(2,1)} %get-tuple-element.41), channel_id=1, source_target_pairs={{0,2},{1,3},{2,0},{3,1},{4,6},{5,7},{6,4},{7,5},{8,10},{9,11},{10,... | collective-permute-start | bytes 1105928 | tf_op jit(solution)/shard_map/ppermute | solution.py:220
  5.7 2.0 %slice-start.1 = ((bf16[1,1440,256]{2,1,0:T(8,128)(2,1)}), bf16[1,8,256]{2,1,0:T(8,128)(2,1)S(1)}, s32[]{:S(2)}) async-start(bf16[1,1440,256]{2,1,0:T(8,128)(2,1)} %param.9), calls=%async_computation.1 | async-start | bytes 8192 | tf_op jit(solution)/shard_map/jit(_roll_static)/slice | solution.py:243
  5.7 2.1 %copy-start = (bf16[2304,256]{1,0:T(8,128)(2,1)S(1)}, bf16[2304,256]{1,0:T(8,128)(2,1)}, u32[]{:S(2)}) copy-start(bf16[2304,256]{1,0:T(8,128)(2,1)} %refs_9_.1) | copy-start | bytes 3538948
  9.4 5.8 %copy-start.2 = (bf16[1,1440,256]{2,1,0:T(8,128)(2,1)S(1)}, bf16[1,1440,256]{2,1,0:T(8,128)(2,1)}, u32[]{:S(2)}) copy-start(bf16[1,1440,256]{2,1,0:T(8,128)(2,1)} %param.9) | copy-start | bytes 2211844
  11.9 15.3 %copy-start.1 = (bf16[1,1440,256]{2,1,0:T(8,128)(2,1)S(1)}, bf16[1,1440,256]{2,1,0:T(8,128)(2,1)}, u32[]{:S(2)}) copy-start(bf16[1,1440,256]{2,1,0:T(8,128)(2,1)} %param.8) | copy-start | bytes 2211844
  15.2 23.6 %copy-start.3 = (bf16[720,256]{1,0:T(8,128)(2,1)}, bf16[720,256]{1,0:T(8,128)(2,1)S(1)}, u32[]{:S(2)}) copy-start(bf16[720,256]{1,0:T(8,128)(2,1)S(1)} %collective-permute-done.refs_2_) | copy-start | bytes 1105924
  15.3 19.0 %collective-permute-start.5 = (bf16[960,256]{1,0:T(8,128)(2,1)S(1)}, bf16[960,256]{1,0:T(8,128)(2,1)}, u32[]{:S(2)}, u32[]{:S(2)}) collective-permute-start(bf16[960,256]{1,0:T(8,128)(2,1)S(1)} %slice.40), channel_id=1, source_target_pairs={{0,2},{1,3},{2,0},{3,1},{4,6},{5,7},{6,4},{7,5},{8,10},{9,11},{10,... | collective-permute-start | bytes 1474568 | tf_op jit(solution)/shard_map/ppermute | solution.py:220
  17.4 10.3 %collective-permute-start.3 = (bf16[720,256]{1,0:T(8,128)(2,1)S(1)}, bf16[720,256]{1,0:T(8,128)(2,1)S(1)}, u32[]{:S(2)}, u32[]{:S(2)}) collective-permute-start(bf16[720,256]{1,0:T(8,128)(2,1)S(1)} %collective-permute-done.refs_2_), channel_id=1, source_target_pairs={{0,4},{1,5},{4,8},{5,9},{8,12},{9,13},{6,2},{7,3},{10,6},{11,7},{1... | collective-permute-start | bytes 1105928 | tf_op jit(solution)/shard_map/ppermute | solution.py:220
  23.1 15.8 %copy-start.4 = (bf16[720,256]{1,0:T(8,128)(2,1)}, bf16[720,256]{1,0:T(8,128)(2,1)S(1)}, u32[]{:S(2)}) copy-start(bf16[720,256]{1,0:T(8,128)(2,1)S(1)} %collective-permute-done.2.refs_3_) | copy-start | bytes 1105924
  23.1 11.2 %collective-permute-start.4 = (bf16[720,256]{1,0:T(8,128)(2,1)S(1)}, bf16[720,256]{1,0:T(8,128)(2,1)S(1)}, u32[]{:S(2)}, u32[]{:S(2)}) collective-permute-start(bf16[720,256]{1,0:T(8,128)(2,1)S(1)} %collective-permute-done.2.refs_3_), channel_id=1, source_target_pairs={{0,4},{1,5},{4,8},{5,9},{8,12},{9,13},{6,2},{7,3},{10,6},{11,7},{1... | collective-permute-start | bytes 1105928 | tf_op jit(solution)/shard_map/ppermute | solution.py:220
  27.2 15.5 %collective-permute-start.1 = (bf16[1440,256]{1,0:T(8,128)(2,1)S(1)}, bf16[1440,256]{1,0:T(8,128)(2,1)}, u32[]{:S(2)}, u32[]{:S(2)}) collective-permute-start(bf16[1440,256]{1,0:T(8,128)(2,1)S(1)} %bitcast.40), channel_id=1, source_target_pairs={{0,1},{1,0},{2,3},{3,2},{4,5},{5,4},{6,7},{7,6},{8,9},{9,8},{10,11... | collective-permute-start | bytes 2211848 | tf_op jit(solution)/shard_map/ppermute | solution.py:220
  27.3 11.9 %collective-permute-start.9 = (bf16[480,256]{1,0:T(8,128)(2,1)S(1)}, bf16[480,256]{1,0:T(8,128)(2,1)}, u32[]{:S(2)}, u32[]{:S(2)}) collective-permute-start(bf16[480,256]{1,0:T(8,128)(2,1)S(1)} %slice.41), channel_id=1, source_target_pairs={{0,2},{1,3},{2,0},{3,1},{4,6},{5,7},{6,4},{7,5},{8,10},{9,11},{10,... | collective-permute-start | bytes 737288 | tf_op jit(solution)/shard_map/ppermute | solution.py:220
  27.6 15.1 %copy-start.5 = (bf16[720,256]{1,0:T(8,128)(2,1)}, bf16[720,256]{1,0:T(8,128)(2,1)S(1)}, u32[]{:S(2)}) copy-start(bf16[720,256]{1,0:T(8,128)(2,1)S(1)} %collective-permute-done.3.refs_4_) | copy-start | bytes 1105924
  34.3 8.4 %copy-start.6 = (bf16[720,256]{1,0:T(8,128)(2,1)}, bf16[720,256]{1,0:T(8,128)(2,1)S(1)}, u32[]{:S(2)}) copy-start(bf16[720,256]{1,0:T(8,128)(2,1)S(1)} %collective-permute-done.4.refs_5_) | copy-start | bytes 1105924
  34.3 8.3 %collective-permute-start.7 = (bf16[720,256]{1,0:T(8,128)(2,1)S(1)}, bf16[720,256]{1,0:T(8,128)(2,1)S(1)}, u32[]{:S(2)}, u32[]{:S(2)}) collective-permute-start(bf16[720,256]{1,0:T(8,128)(2,1)S(1)} %broadcast_select_fusion.1), channel_id=1, source_target_pairs={{0,1},{1,0},{2,3},{3,2},{4,5},{5,4},{6,7},{7,6},{8,9},{9,8},{10,11... | collective-permute-start | bytes 1105928 | tf_op jit(solution)/shard_map/ppermute | solution.py:220
  34.4 21.7 %collective-permute-start.8 = (bf16[960,256]{1,0:T(8,128)(2,1)}, bf16[960,256]{1,0:T(8,128)(2,1)S(1)}, u32[]{:S(2)}, u32[]{:S(2)}) collective-permute-start(bf16[960,256]{1,0:T(8,128)(2,1)} %collective-permute-done.5.refs_2_), channel_id=1, source_target_pairs={{0,4},{1,5},{4,8},{5,9},{8,12},{9,13},{6,2},{7,3},{10,6},{11,7},{1... | collective-permute-start | bytes 1474568 | tf_op jit(solution)/shard_map/ppermute | solution.py:220
  38.9 3.8 %collective-permute-start.6 = (bf16[720,256]{1,0:T(8,128)(2,1)S(1)}, bf16[720,256]{1,0:T(8,128)(2,1)S(1)}, u32[]{:S(2)}, u32[]{:S(2)}) collective-permute-start(bf16[720,256]{1,0:T(8,128)(2,1)S(1)} %broadcast_select_fusion.2), channel_id=1, source_target_pairs={{0,1},{1,0},{2,3},{3,2},{4,5},{5,4},{6,7},{7,6},{8,9},{9,8},{10,11... | collective-permute-start | bytes 1105928 | tf_op jit(solution)/shard_map/ppermute | solution.py:220
  39.2 16.9 %collective-permute-start.10 = (bf16[480,256]{1,0:T(8,128)(2,1)}, bf16[480,256]{1,0:T(8,128)(2,1)S(1)}, u32[]{:S(2)}, u32[]{:S(2)}) collective-permute-start(bf16[480,256]{1,0:T(8,128)(2,1)} %collective-permute-done.9.refs_3_), channel_id=1, source_target_pairs={{0,4},{1,5},{4,8},{5,9},{8,12},{9,13},{6,2},{7,3},{10,6},{11,7},{1... | collective-permute-start | bytes 737288 | tf_op jit(solution)/shard_map/ppermute | solution.py:220
  42.7 0.8 copy-start.9
  43.4 0.8 copy-start.10
  56.0 2.9 %copy-start.7 = (bf16[8,144,256]{2,1,0:T(8,128)(2,1)S(1)}, bf16[8,144,256]{2,1,0:T(8,128)(2,1)}, u32[]{:S(2)}) copy-start(bf16[8,144,256]{2,1,0:T(8,128)(2,1)} %get-tuple-element.32) | copy-start | bytes 1769476
  56.1 3.0 %copy-start.11 = (bf16[480,256]{1,0:T(8,128)(2,1)}, bf16[480,256]{1,0:T(8,128)(2,1)S(1)}, u32[]{:S(2)}) copy-start(bf16[480,256]{1,0:T(8,128)(2,1)S(1)} %collective-permute-done.10.refs_5_) | copy-start | bytes 737284
  56.1 3.0 %copy-start.8 = (bf16[960,256]{1,0:T(8,128)(2,1)}, bf16[960,256]{1,0:T(8,128)(2,1)S(1)}, u32[]{:S(2)}) copy-start(bf16[960,256]{1,0:T(8,128)(2,1)S(1)} %collective-permute-done.8.refs_4_) | copy-start | bytes 1474564
  56.1 2.8 %collective-permute-start.11 = (bf16[8,144,256]{2,1,0:T(8,128)(2,1)}, bf16[8,144,256]{2,1,0:T(8,128)(2,1)S(1)}, u32[]{:S(2)}, u32[]{:S(2)}) collective-permute-start(bf16[8,144,256]{2,1,0:T(8,128)(2,1)} %get-tuple-element.34), channel_id=1, source_target_pairs={{0,1},{1,0},{2,3},{3,2},{4,5},{5,4},{6,7},{7,6},{8,9},{9,8},{10,11... | collective-permute-start | bytes 1769480 | tf_op jit(solution)/shard_map/ppermute | solution.py:220
  56.2 3.9 %collective-permute-start.13 = (bf16[1440,256]{1,0:T(8,128)(2,1)S(1)}, bf16[1440,256]{1,0:T(8,128)(2,1)}, u32[]{:S(2)}, u32[]{:S(2)}) collective-permute-start(bf16[1440,256]{1,0:T(8,128)(2,1)S(1)} %bitcast.44), channel_id=1, source_target_pairs={{0,1},{1,0},{2,3},{3,2},{4,5},{5,4},{6,7},{7,6},{8,9},{9,8},{10,11... | collective-permute-start | bytes 2211848 | tf_op jit(solution)/shard_map/ppermute | solution.py:220
  57.8 2.7 %collective-permute-start.14 = (bf16[960,256]{1,0:T(8,128)(2,1)S(1)}, bf16[960,256]{1,0:T(8,128)(2,1)}, u32[]{:S(2)}, u32[]{:S(2)}) collective-permute-start(bf16[960,256]{1,0:T(8,128)(2,1)S(1)} %broadcast_select_fusion), channel_id=1, source_target_pairs={{0,1},{1,0},{2,3},{3,2},{4,5},{5,4},{6,7},{7,6},{8,9},{9,8},{10,11... | collective-permute-start | bytes 1474568 | tf_op jit(solution)/shard_map/ppermute | solution.py:220
  58.8 1.6 %collective-permute-start.15 = (bf16[480,256]{1,0:T(8,128)(2,1)S(1)}, bf16[480,256]{1,0:T(8,128)(2,1)S(1)}, u32[]{:S(2)}, u32[]{:S(2)}) collective-permute-start(bf16[480,256]{1,0:T(8,128)(2,1)S(1)} %broadcast_select_fusion.3), channel_id=1, source_target_pairs={{0,1},{1,0},{2,3},{3,2},{4,5},{5,4},{6,7},{7,6},{8,9},{9,8},{10,11... | collective-permute-start | bytes 737288 | tf_op jit(solution)/shard_map/ppermute | solution.py:220
  59.1 11.3 %collective-permute-start.12 = (bf16[4,144,256]{2,1,0:T(8,128)(2,1)S(1)}, bf16[4,144,256]{2,1,0:T(8,128)(2,1)S(1)}, u32[]{:S(2)}, u32[]{:S(2)}) collective-permute-start(bf16[4,144,256]{2,1,0:T(8,128)(2,1)S(1)} %dynamic-slice_bitcast_fusion), channel_id=1, source_target_pairs={{0,2},{1,3},{2,0},{3,1},{4,6},{5,7},{6,4},{7,5},{8,10},{9,11},{10,... | collective-permute-start | bytes 884744 | tf_op jit(solution)/shard_map/ppermute | solution.py:220
  60.4 0.7 copy-start.14
  70.5 6.0 %collective-permute-start.16 = (bf16[2,144,256]{2,1,0:T(8,128)(2,1)S(1)}, bf16[2,144,256]{2,1,0:T(8,128)(2,1)S(1)}, u32[]{:S(2)}, u32[]{:S(2)}) collective-permute-start(bf16[2,144,256]{2,1,0:T(8,128)(2,1)S(1)} %dynamic-slice_bitcast_fusion.1), channel_id=1, source_target_pairs={{0,4},{1,5},{2,6},{3,7},{4,0},{5,1},{6,2},{7,3},{8,12},{9,13},{10,... | collective-permute-start | bytes 442376 | tf_op jit(solution)/shard_map/ppermute | solution.py:220
  76.6 5.6 %collective-permute-start.17 = (bf16[1,144,256]{2,1,0:T(8,128)(2,1)S(1)}, bf16[1,144,256]{2,1,0:T(8,128)(2,1)S(1)}, u32[]{:S(2)}, u32[]{:S(2)}) collective-permute-start(bf16[1,144,256]{2,1,0:T(8,128)(2,1)S(1)} %constant_dynamic-slice_fusion), channel_id=1, source_target_pairs={{0,8},{1,9},{2,10},{3,11},{4,12},{5,13},{6,14},{7,15},{8,0},{9,1},... | collective-permute-start | bytes 221192 | tf_op jit(solution)/shard_map/ppermute | solution.py:220

commit v4 on v3

--- a/solution.py
+++ b/solution.py
@@ -109,7 +109,7 @@
 def mix(band, slots, mixed, begin, blocks):
     width = slots.shape[2]
 
-    @pl.loop(0, blocks, unroll=5)
+    @pl.loop(0, blocks, unroll=15)
     def _(block):
         at = pl.multiple_of(begin + block * BLOCK, BLOCK)
         window = jnp.concatenate([slots[slot, pl.ds(at, WINDOW), :] for slot in range(DEPTH)], axis=0)
@@ -136,13 +136,13 @@
     for copies in groups[1:]:
         for copy in copies:
             copy.start()
+    for copies in groups:
+        for copy in copies:
+            copy.wait()
+    mix(band, slots, mixed, 0, cells // BLOCK)
+    for copy in fetches:
+        copy.wait()
     for part in range(TILES):
-        for copy in groups[part]:
-            copy.wait()
-        mix(band, slots, mixed, part * tile, tile // BLOCK)
-        if part == 0:
-            for copy in fetches:
-                copy.wait()
         shifted[part * tile + SHIFT : (part + 1) * tile + SHIFT] = jnp.dot(
             mixed[part * tile : (part + 1) * tile], weights[...], preferred_element_type=jnp.float32
         )

time: 83.3 us -> 82.9 us (level)
    pallas_call x2, Pallas kernels: 21.1 us -> 20.3 us  [layer(): pl.pallas_call(functools.partial(layer_kernel, counts), out_shape=outs, i...]
  transfers between devices with their start and end apart: 18 -> 18, of which waited for: 7 -> 6; matrix products, arithmetic and copies ran while one was open for 9% -> 9% of each run, Pallas kernels for 28% -> 27%
where the time goes in v4:
time: 82.9 us; the launch traced here: 82.5 us
  starting transfers between devices  28.2 us (34%)
  Pallas kernels  22.2 us (27%)
  waiting for transfers between devices  18.4 us (22%)
  local copies, waits for them, and re-layouts  8.65 us (10%)
  other arithmetic  4.1 us (5%)
  between operations  1.01 us (1%)
    ppermute x18, starting transfers between devices, sent(): return lax.ppermute(array, 'lat', pairs)  28.2 us
    pallas_call x2, Pallas kernels, layer(): pl.pallas_call(functools.partial(layer_kernel, counts), out_shape=outs, i...  20.3 us
    ppermute x18, waiting for transfers between devices, sent(): return lax.ppermute(array, 'lat', pairs)  18.4 us
    unnamed x34, local copies, waits for them, and re-layouts  2.84 us
    select_n x4, other arithmetic, swapped(): jnp.where(side == core, one, other)  2.15 us
    slice x3, local copies, waits for them, and re-layouts, split(): return [row[low:high] for low, high in zip(edges, edges[1:])]  2.06 us
    pallas_call x1, Pallas kernels, bands(): pl.pallas_call(bands_kernel, out_shape=[jax.ShapeDtypeStruct(BAND, jnp.bf...  1.91 us
  transfers between devices with their start and end apart: 18, of which 6 were waited for; matrix products, arithmetic and copies ran while one was open for 9% of the time, Pallas kernels for 27%

profile of v4, /device:TPU:0, one launch (start us, length us, event | category | flops | bytes accessed | tf_op | source)
XLA Modules:
  0.0 82.5 jit_solution(9754088675630559614)
XLA Ops:
  0.6 2.0 %slice_bitcast_fusion = (bf16[720,256]{1,0:T(8,128)(2,1)}, bf16[720,256]{1,0:T(8,128)(2,1)}) fusion(bf16[1,1440,256]{2,1,0:T(8,128)(2,1)} %param.8), kind=kLoop, calls=%fused_computation.5 | loop fusion | bytes 1474560 | tf_op jit(solution)/shard_map/slice | solution.py:237
  2.7 2.9 %collective-permute-start = (bf16[720,256]{1,0:T(8,128)(2,1)}, bf16[720,256]{1,0:T(8,128)(2,1)S(1)}, u32[]{:S(2)}, u32[]{:S(2)}) collective-permute-start(bf16[720,256]{1,0:T(8,128)(2,1)} %get-tuple-element.42), channel_id=1, source_target_pairs={{0,2},{1,3},{2,0},{3,1},{4,6},{5,7},{6,4},{7,5},{8,10},{9,11},{10,... | collective-permute-start | bytes 1105928 | tf_op jit(solution)/shard_map/ppermute | solution.py:220
  5.6 0.1 collective-permute-start.2
  5.7 0.0 copy-done.12
  5.7 0.1 copy.17
  5.8 0.7 reshape.43.basis
  6.5 0.1 copy.18
  6.7 0.7 reshape.44.quad
  7.4 0.3 copy.20
  7.7 0.1 copy.21
  7.8 1.6 %copy.16 = bf16[9,256,256]{1,2,0:T(8,128)(2,1)} copy(bf16[9,256,256]{2,1,0:T(8,128)(2,1)S(1)} %bitcast.37) | data formatting | bytes 2359296 | tf_op jit(solution)/shard_map/reshape | solution.py:244
  9.4 0.6 stack.23.meta
  10.0 1.9 %bands.1 = (bf16[288,240]{1,0:T(8,128)(2,1)}, bf16[288,240]{1,0:T(8,128)(2,1)}) custom-call(s32[7]{0:T(128)} %stack.23.meta, s32[16]{0:T(128)} %first.1, s32[16]{0:T(128)} %last.1, s32[16]{0:T(128)} %reach.1, s32[560]{0:T(1024)} %reshape.43.basis, f32[560]{0:T(1024)} %reshape.44.quad), custom_call_target="tpu_custom_call" | custom-call | tf_op jit(solution)/shard_map/bands/pallas_call | solution.py:71
  11.9 1.0 %maximum_bitcast_fusion.refs_10_ = bf16[256,1440]{1,0:T(8,128)(2,1)} fusion(bf16[8,256]{0,1:T(8,128)(2,1)S(1)} %bitcast.50, bf16[1432,256]{0,1:T(8,128)(2,1)S(1)} %bitcast.38), kind=kLoop, calls=%fused_computation.1 | loop fusion | flops 1474560 | bytes 1474560 | tf_op jit(solution)/shard_map/transpose | solution.py:243
  12.9 2.3 %collective-permute-done.refs_2_ = bf16[720,256]{1,0:T(8,128)(2,1)S(1)} collective-permute-done((bf16[720,256]{1,0:T(8,128)(2,1)}, bf16[720,256]{1,0:T(8,128)(2,1)S(1)}, u32[]{:S(2)}, u32[]{:S(2)}) %collective-permute-start) | collective-permute-done | bytes 368672 | tf_op jit(solution)/shard_map/ppermute | solution.py:220
  15.3 2.1 %collective-permute-start.5 = (bf16[960,256]{1,0:T(8,128)(2,1)S(1)}, bf16[960,256]{1,0:T(8,128)(2,1)}, u32[]{:S(2)}, u32[]{:S(2)}) collective-permute-start(bf16[960,256]{1,0:T(8,128)(2,1)S(1)} %slice.40), channel_id=1, source_target_pairs={{0,2},{1,3},{2,0},{3,1},{4,6},{5,7},{6,4},{7,5},{8,10},{9,11},{10,... | collective-permute-start | bytes 1474568 | tf_op jit(solution)/shard_map/ppermute | solution.py:220
  17.4 3.5 %collective-permute-start.3 = (bf16[720,256]{1,0:T(8,128)(2,1)S(1)}, bf16[720,256]{1,0:T(8,128)(2,1)S(1)}, u32[]{:S(2)}, u32[]{:S(2)}) collective-permute-start(bf16[720,256]{1,0:T(8,128)(2,1)S(1)} %collective-permute-done.refs_2_), channel_id=1, source_target_pairs={{0,4},{1,5},{4,8},{5,9},{8,12},{9,13},{6,2},{7,3},{10,6},{11,7},{1... | collective-permute-start | bytes 1105928 | tf_op jit(solution)/shard_map/ppermute | solution.py:220
  20.9 2.2 %collective-permute-done.2.refs_3_ = bf16[720,256]{1,0:T(8,128)(2,1)S(1)} collective-permute-done((bf16[720,256]{1,0:T(8,128)(2,1)}, bf16[720,256]{1,0:T(8,128)(2,1)S(1)}, u32[]{:S(2)}, u32[]{:S(2)}) %collective-permute-start.2) | collective-permute-done | bytes 368672 | tf_op jit(solution)/shard_map/ppermute | solution.py:220
  23.1 4.1 %collective-permute-start.4 = (bf16[720,256]{1,0:T(8,128)(2,1)S(1)}, bf16[720,256]{1,0:T(8,128)(2,1)S(1)}, u32[]{:S(2)}, u32[]{:S(2)}) collective-permute-start(bf16[720,256]{1,0:T(8,128)(2,1)S(1)} %collective-permute-done.2.refs_3_), channel_id=1, source_target_pairs={{0,4},{1,5},{4,8},{5,9},{8,12},{9,13},{6,2},{7,3},{10,6},{11,7},{1... | collective-permute-start | bytes 1105928 | tf_op jit(solution)/shard_map/ppermute | solution.py:220
  27.2 0.1 collective-permute-start.1
  27.3 0.1 collective-permute-start.9
  27.4 0.2 collective-permute-done.3.refs_4_
  27.6 6.7 %collective-permute-done.4.refs_5_ = bf16[720,256]{1,0:T(8,128)(2,1)S(1)} collective-permute-done((bf16[720,256]{1,0:T(8,128)(2,1)S(1)}, bf16[720,256]{1,0:T(8,128)(2,1)S(1)}, u32[]{:S(2)}, u32[]{:S(2)}) %collective-permute-start.4) | collective-permute-done | bytes 368672 | tf_op jit(solution)/shard_map/ppermute | solution.py:220
  34.3 0.0 collective-permute-done.5.refs_2_
  34.3 0.1 collective-permute-start.7
  34.4 4.4 %collective-permute-start.8 = (bf16[960,256]{1,0:T(8,128)(2,1)}, bf16[960,256]{1,0:T(8,128)(2,1)S(1)}, u32[]{:S(2)}, u32[]{:S(2)}) collective-permute-start(bf16[960,256]{1,0:T(8,128)(2,1)} %collective-permute-done.5.refs_2_), channel_id=1, source_target_pairs={{0,4},{1,5},{4,8},{5,9},{8,12},{9,13},{6,2},{7,3},{10,6},{11,7},{1... | collective-permute-start | bytes 1474568 | tf_op jit(solution)/shard_map/ppermute | solution.py:220
  38.9 0.3 collective-permute-start.6
  39.2 0.0 collective-permute-done.9.refs_3_
  39.2 3.5 %collective-permute-start.10 = (bf16[480,256]{1,0:T(8,128)(2,1)}, bf16[480,256]{1,0:T(8,128)(2,1)S(1)}, u32[]{:S(2)}, u32[]{:S(2)}) collective-permute-start(bf16[480,256]{1,0:T(8,128)(2,1)} %collective-permute-done.9.refs_3_), channel_id=1, source_target_pairs={{0,4},{1,5},{4,8},{5,9},{8,12},{9,13},{6,2},{7,3},{10,6},{11,7},{1... | collective-permute-start | bytes 737288 | tf_op jit(solution)/shard_map/ppermute | solution.py:220
  42.7 0.0 collective-permute-done.1.refs_1_
  42.7 0.0 collective-permute-done.7.refs_7_
  42.7 0.0 collective-permute-done.6.refs_6_
  42.7 0.0 copy-done.5
  42.7 0.0 copy-done.6
  42.7 0.7 copy-done.9
  43.4 0.7 copy-done.10
  44.2 11.4 %forward_layer.1 = (bf16[1440,256]{1,0:T(8,128)(2,1)}, bf16[8,144,256]{2,1,0:T(8,128)(2,1)}, bf16[8,144,256]{2,1,0:T(8,128)(2,1)}) custom-call(s32[7]{0:T(128)} %stack.23.meta, bf16[1440,256]{1,0:T(8,128)(2,1)} %bitcast.39, bf16[1440,256]{1,0:T(8,128)(2,1)} %collective-permute-done.1.refs_1_, bf16[720,256]{1,0:T(8,128)(2,1)} %copy-done.3, ...), custom_call_target="tpu_custom_call" | custom-call | flops 1 | tf_op jit(solution)/shard_map/forward_layer/pallas_call | solution.py:182
  55.6 0.0 copy-start.7
  55.6 0.0 collective-permute-done.10.refs_5_
  55.6 0.0 copy-start.11
  55.6 0.0 collective-permute-done.8.refs_4_
  55.6 0.1 collective-permute-start.11
  55.7 0.5 collective-permute-start.13
  56.2 1.1 %broadcast_select_fusion = bf16[960,256]{1,0:T(8,128)(2,1)S(1)} fusion(bf16[960,256]{1,0:T(8,128)(2,1)} %collective-permute-done.5.refs_2_, bf16[960,256]{1,0:T(8,128)(2,1)S(1)} %collective-permute-done.8.refs_4_, pred[]{:T(512)S(6)} %eq.22), kind=kLoop, calls=%fused_computation.4 | loop fusion | flops 245760 | bytes 1474561 | tf_op jit(solution)/shard_map/jit(_where)/select_n | solution.py:240
  57.3 0.1 collective-permute-start.14
  57.4 1.0 %broadcast_select_fusion.3 = bf16[480,256]{1,0:T(8,128)(2,1)S(1)} fusion(bf16[480,256]{1,0:T(8,128)(2,1)} %collective-permute-done.9.refs_3_, bf16[480,256]{1,0:T(8,128)(2,1)S(1)} %collective-permute-done.10.refs_5_, pred[]{:T(512)S(6)} %eq.22), kind=kLoop, calls=%fused_computation.12 | loop fusion | flops 122880 | bytes 737281 | tf_op jit(solution)/shard_map/jit(_where)/select_n | solution.py:240
  58.3 0.1 collective-permute-start.15
  58.4 0.0 collective-permute-done.11
  58.4 0.1 add_convert_fusion
  58.6 0.0 copy-done.11
  58.6 0.0 copy-done.8
  58.7 1.4 %collective-permute-start.12 = (bf16[4,144,256]{2,1,0:T(8,128)(2,1)S(1)}, bf16[4,144,256]{2,1,0:T(8,128)(2,1)S(1)}, u32[]{:S(2)}, u32[]{:S(2)}) collective-permute-start(bf16[4,144,256]{2,1,0:T(8,128)(2,1)S(1)} %dynamic-slice_bitcast_fusion), channel_id=1, source_target_pairs={{0,2},{1,3},{2,0},{3,1},{4,6},{5,7},{6,4},{7,5},{8,10},{9,11},{10,... | collective-permute-start | bytes 884744 | tf_op jit(solution)/shard_map/ppermute | solution.py:220
  60.1 0.0 collective-permute-done.13.refs_1_
  60.1 0.0 collective-permute-done.15.refs_7_
  60.1 0.0 collective-permute-done.14.refs_6_
  60.1 0.7 copy-done.14
  60.8 8.9 %backward_layer.1 = bf16[1440,256]{1,0:T(8,128)(2,1)} custom-call(s32[7]{0:T(128)} %stack.23.meta, bf16[1440,256]{1,0:T(8,128)(2,1)} %bitcast.41, bf16[1440,256]{1,0:T(8,128)(2,1)} %collective-permute-done.13.refs_1_, bf16[960,256]{1,0:T(8,128)(2,1)} %collective-permute-done.5.refs_2_, bf16[480,256]{1,0:T(8,128)(2,1)} %collective-permute-done.9.refs_3_, ...), custom_call_target="tpu_custom_call" | custom-call | flops 5000000000 | bytes 50000000 | tf_op jit(solution)/shard_map/backward_layer/pallas_call | solution.py:182
  69.7 0.0 collective-permute-done.12
  69.7 0.1 fusion
  69.8 2.2 %collective-permute-start.16 = (bf16[2,144,256]{2,1,0:T(8,128)(2,1)S(1)}, bf16[2,144,256]{2,1,0:T(8,128)(2,1)S(1)}, u32[]{:S(2)}, u32[]{:S(2)}) collective-permute-start(bf16[2,144,256]{2,1,0:T(8,128)(2,1)S(1)} %dynamic-slice_bitcast_fusion.1), channel_id=1, source_target_pairs={{0,4},{1,5},{2,6},{3,7},{4,0},{5,1},{6,2},{7,3},{8,12},{9,13},{10,... | collective-permute-start | bytes 442376 | tf_op jit(solution)/shard_map/ppermute | solution.py:220
  72.0 4.2 %collective-permute-done.16 = bf16[2,144,256]{2,1,0:T(8,128)(2,1)S(1)} collective-permute-done((bf16[2,144,256]{2,1,0:T(8,128)(2,1)S(1)}, bf16[2,144,256]{2,1,0:T(8,128)(2,1)S(1)}, u32[]{:S(2)}, u32[]{:S(2)}) %collective-permute-start.16) | collective-permute-done | bytes 147488 | tf_op jit(solution)/shard_map/ppermute | solution.py:220
  76.2 2.8 %collective-permute-start.17 = (bf16[1,144,256]{2,1,0:T(8,128)(2,1)S(1)}, bf16[1,144,256]{2,1,0:T(8,128)(2,1)S(1)}, u32[]{:S(2)}, u32[]{:S(2)}) collective-permute-start(bf16[1,144,256]{2,1,0:T(8,128)(2,1)S(1)} %constant_dynamic-slice_fusion), channel_id=1, source_target_pairs={{0,8},{1,9},{2,10},{3,11},{4,12},{5,13},{6,14},{7,15},{8,0},{9,1},... | collective-permute-start | bytes 221192 | tf_op jit(solution)/shard_map/ppermute | solution.py:220
  79.0 2.8 %collective-permute-done.17 = bf16[1,144,256]{2,1,0:T(8,128)(2,1)S(1)} collective-permute-done((bf16[1,144,256]{2,1,0:T(8,128)(2,1)S(1)}, bf16[1,144,256]{2,1,0:T(8,128)(2,1)S(1)}, u32[]{:S(2)}, u32[]{:S(2)}) %collective-permute-start.17) | collective-permute-done | bytes 73760 | tf_op jit(solution)/shard_map/ppermute | solution.py:220
  81.8 0.7 multiply_bitcast_fusion
  (32 shorter events, 0.3 us)
Async XLA Ops:
  0.6 5.0 %copy-start.12 = (s32[16,5,7]{0,2,1:T(8,128)S(1)}, s32[16,5,7]{0,2,1:T(8,128)}, u32[]{:S(2)}) copy-start(s32[16,5,7]{0,2,1:T(8,128)} %param.14) | copy-start | bytes 6724
  2.7 3.9 %copy-start.13 = (f32[16,5,7]{0,2,1:T(8,128)S(1)}, f32[16,5,7]{0,2,1:T(8,128)}, u32[]{:S(2)}) copy-start(f32[16,5,7]{0,2,1:T(8,128)} %param.15) | copy-start | bytes 6724
  2.7 4.7 %slice-start = ((bf16[1,1440,256]{2,1,0:T(8,128)(2,1)}), bf16[1,1432,256]{2,1,0:T(8,128)(2,1)S(1)}, s32[]{:S(2)}) async-start(bf16[1,1440,256]{2,1,0:T(8,128)(2,1)} %param.9), calls=%async_computation | async-start | bytes 1466368 | tf_op jit(solution)/shard_map/jit(_roll_static)/slice | solution.py:243
  2.7 12.6 %collective-permute-start = (bf16[720,256]{1,0:T(8,128)(2,1)}, bf16[720,256]{1,0:T(8,128)(2,1)S(1)}, u32[]{:S(2)}, u32[]{:S(2)}) collective-permute-start(bf16[720,256]{1,0:T(8,128)(2,1)} %get-tuple-element.42), channel_id=1, source_target_pairs={{0,2},{1,3},{2,0},{3,1},{4,6},{5,7},{6,4},{7,5},{8,10},{9,11},{10,... | collective-permute-start | bytes 1105928 | tf_op jit(solution)/shard_map/ppermute | solution.py:220
  5.6 17.5 %collective-permute-start.2 = (bf16[720,256]{1,0:T(8,128)(2,1)}, bf16[720,256]{1,0:T(8,128)(2,1)S(1)}, u32[]{:S(2)}, u32[]{:S(2)}) collective-permute-start(bf16[720,256]{1,0:T(8,128)(2,1)} %get-tuple-element.41), channel_id=1, source_target_pairs={{0,2},{1,3},{2,0},{3,1},{4,6},{5,7},{6,4},{7,5},{8,10},{9,11},{10,... | collective-permute-start | bytes 1105928 | tf_op jit(solution)/shard_map/ppermute | solution.py:220
  5.7 2.0 %slice-start.1 = ((bf16[1,1440,256]{2,1,0:T(8,128)(2,1)}), bf16[1,8,256]{2,1,0:T(8,128)(2,1)S(1)}, s32[]{:S(2)}) async-start(bf16[1,1440,256]{2,1,0:T(8,128)(2,1)} %param.9), calls=%async_computation.1 | async-start | bytes 8192 | tf_op jit(solution)/shard_map/jit(_roll_static)/slice | solution.py:243
  5.7 2.1 %copy-start = (bf16[2304,256]{1,0:T(8,128)(2,1)S(1)}, bf16[2304,256]{1,0:T(8,128)(2,1)}, u32[]{:S(2)}) copy-start(bf16[2304,256]{1,0:T(8,128)(2,1)} %refs_9_.1) | copy-start | bytes 3538948
  9.4 5.8 %copy-start.2 = (bf16[1,1440,256]{2,1,0:T(8,128)(2,1)S(1)}, bf16[1,1440,256]{2,1,0:T(8,128)(2,1)}, u32[]{:S(2)}) copy-start(bf16[1,1440,256]{2,1,0:T(8,128)(2,1)} %param.9) | copy-start | bytes 2211844
  11.9 15.3 %copy-start.1 = (bf16[1,1440,256]{2,1,0:T(8,128)(2,1)S(1)}, bf16[1,1440,256]{2,1,0:T(8,128)(2,1)}, u32[]{:S(2)}) copy-start(bf16[1,1440,256]{2,1,0:T(8,128)(2,1)} %param.8) | copy-start | bytes 2211844
  15.2 23.6 %copy-start.3 = (bf16[720,256]{1,0:T(8,128)(2,1)}, bf16[720,256]{1,0:T(8,128)(2,1)S(1)}, u32[]{:S(2)}) copy-start(bf16[720,256]{1,0:T(8,128)(2,1)S(1)} %collective-permute-done.refs_2_) | copy-start | bytes 1105924
  15.3 19.0 %collective-permute-start.5 = (bf16[960,256]{1,0:T(8,128)(2,1)S(1)}, bf16[960,256]{1,0:T(8,128)(2,1)}, u32[]{:S(2)}, u32[]{:S(2)}) collective-permute-start(bf16[960,256]{1,0:T(8,128)(2,1)S(1)} %slice.40), channel_id=1, source_target_pairs={{0,2},{1,3},{2,0},{3,1},{4,6},{5,7},{6,4},{7,5},{8,10},{9,11},{10,... | collective-permute-start | bytes 1474568 | tf_op jit(solution)/shard_map/ppermute | solution.py:220
  17.4 10.3 %collective-permute-start.3 = (bf16[720,256]{1,0:T(8,128)(2,1)S(1)}, bf16[720,256]{1,0:T(8,128)(2,1)S(1)}, u32[]{:S(2)}, u32[]{:S(2)}) collective-permute-start(bf16[720,256]{1,0:T(8,128)(2,1)S(1)} %collective-permute-done.refs_2_), channel_id=1, source_target_pairs={{0,4},{1,5},{4,8},{5,9},{8,12},{9,13},{6,2},{7,3},{10,6},{11,7},{1... | collective-permute-start | bytes 1105928 | tf_op jit(solution)/shard_map/ppermute | solution.py:220
  23.1 15.8 %copy-start.4 = (bf16[720,256]{1,0:T(8,128)(2,1)}, bf16[720,256]{1,0:T(8,128)(2,1)S(1)}, u32[]{:S(2)}) copy-start(bf16[720,256]{1,0:T(8,128)(2,1)S(1)} %collective-permute-done.2.refs_3_) | copy-start | bytes 1105924
  23.1 11.2 %collective-permute-start.4 = (bf16[720,256]{1,0:T(8,128)(2,1)S(1)}, bf16[720,256]{1,0:T(8,128)(2,1)S(1)}, u32[]{:S(2)}, u32[]{:S(2)}) collective-permute-start(bf16[720,256]{1,0:T(8,128)(2,1)S(1)} %collective-permute-done.2.refs_3_), channel_id=1, source_target_pairs={{0,4},{1,5},{4,8},{5,9},{8,12},{9,13},{6,2},{7,3},{10,6},{11,7},{1... | collective-permute-start | bytes 1105928 | tf_op jit(solution)/shard_map/ppermute | solution.py:220
  27.2 15.5 %collective-permute-start.1 = (bf16[1440,256]{1,0:T(8,128)(2,1)S(1)}, bf16[1440,256]{1,0:T(8,128)(2,1)}, u32[]{:S(2)}, u32[]{:S(2)}) collective-permute-start(bf16[1440,256]{1,0:T(8,128)(2,1)S(1)} %bitcast.40), channel_id=1, source_target_pairs={{0,1},{1,0},{2,3},{3,2},{4,5},{5,4},{6,7},{7,6},{8,9},{9,8},{10,11... | collective-permute-start | bytes 2211848 | tf_op jit(solution)/shard_map/ppermute | solution.py:220
  27.3 11.9 %collective-permute-start.9 = (bf16[480,256]{1,0:T(8,128)(2,1)S(1)}, bf16[480,256]{1,0:T(8,128)(2,1)}, u32[]{:S(2)}, u32[]{:S(2)}) collective-permute-start(bf16[480,256]{1,0:T(8,128)(2,1)S(1)} %slice.41), channel_id=1, source_target_pairs={{0,2},{1,3},{2,0},{3,1},{4,6},{5,7},{6,4},{7,5},{8,10},{9,11},{10,... | collective-permute-start | bytes 737288 | tf_op jit(solution)/shard_map/ppermute | solution.py:220
  27.6 15.1 %copy-start.5 = (bf16[720,256]{1,0:T(8,128)(2,1)}, bf16[720,256]{1,0:T(8,128)(2,1)S(1)}, u32[]{:S(2)}) copy-start(bf16[720,256]{1,0:T(8,128)(2,1)S(1)} %collective-permute-done.3.refs_4_) | copy-start | bytes 1105924
  34.3 8.4 %copy-start.6 = (bf16[720,256]{1,0:T(8,128)(2,1)}, bf16[720,256]{1,0:T(8,128)(2,1)S(1)}, u32[]{:S(2)}) copy-start(bf16[720,256]{1,0:T(8,128)(2,1)S(1)} %collective-permute-done.4.refs_5_) | copy-start | bytes 1105924
  34.3 8.3 %collective-permute-start.7 = (bf16[720,256]{1,0:T(8,128)(2,1)S(1)}, bf16[720,256]{1,0:T(8,128)(2,1)S(1)}, u32[]{:S(2)}, u32[]{:S(2)}) collective-permute-start(bf16[720,256]{1,0:T(8,128)(2,1)S(1)} %broadcast_select_fusion.1), channel_id=1, source_target_pairs={{0,1},{1,0},{2,3},{3,2},{4,5},{5,4},{6,7},{7,6},{8,9},{9,8},{10,11... | collective-permute-start | bytes 1105928 | tf_op jit(solution)/shard_map/ppermute | solution.py:220
  34.4 21.2 %collective-permute-start.8 = (bf16[960,256]{1,0:T(8,128)(2,1)}, bf16[960,256]{1,0:T(8,128)(2,1)S(1)}, u32[]{:S(2)}, u32[]{:S(2)}) collective-permute-start(bf16[960,256]{1,0:T(8,128)(2,1)} %collective-permute-done.5.refs_2_), channel_id=1, source_target_pairs={{0,4},{1,5},{4,8},{5,9},{8,12},{9,13},{6,2},{7,3},{10,6},{11,7},{1... | collective-permute-start | bytes 1474568 | tf_op jit(solution)/shard_map/ppermute | solution.py:220
  38.9 3.8 %collective-permute-start.6 = (bf16[720,256]{1,0:T(8,128)(2,1)S(1)}, bf16[720,256]{1,0:T(8,128)(2,1)S(1)}, u32[]{:S(2)}, u32[]{:S(2)}) collective-permute-start(bf16[720,256]{1,0:T(8,128)(2,1)S(1)} %broadcast_select_fusion.2), channel_id=1, source_target_pairs={{0,1},{1,0},{2,3},{3,2},{4,5},{5,4},{6,7},{7,6},{8,9},{9,8},{10,11... | collective-permute-start | bytes 1105928 | tf_op jit(solution)/shard_map/ppermute | solution.py:220
  39.2 16.4 %collective-permute-start.10 = (bf16[480,256]{1,0:T(8,128)(2,1)}, bf16[480,256]{1,0:T(8,128)(2,1)S(1)}, u32[]{:S(2)}, u32[]{:S(2)}) collective-permute-start(bf16[480,256]{1,0:T(8,128)(2,1)} %collective-permute-done.9.refs_3_), channel_id=1, source_target_pairs={{0,4},{1,5},{4,8},{5,9},{8,12},{9,13},{6,2},{7,3},{10,6},{11,7},{1... | collective-permute-start | bytes 737288 | tf_op jit(solution)/shard_map/ppermute | solution.py:220
  42.7 0.8 copy-start.9
  43.4 0.8 copy-start.10
  55.6 2.9 %copy-start.7 = (bf16[8,144,256]{2,1,0:T(8,128)(2,1)S(1)}, bf16[8,144,256]{2,1,0:T(8,128)(2,1)}, u32[]{:S(2)}) copy-start(bf16[8,144,256]{2,1,0:T(8,128)(2,1)} %get-tuple-element.32) | copy-start | bytes 1769476
  55.6 3.0 %copy-start.11 = (bf16[480,256]{1,0:T(8,128)(2,1)}, bf16[480,256]{1,0:T(8,128)(2,1)S(1)}, u32[]{:S(2)}) copy-start(bf16[480,256]{1,0:T(8,128)(2,1)S(1)} %collective-permute-done.10.refs_5_) | copy-start | bytes 737284
  55.6 3.0 %copy-start.8 = (bf16[960,256]{1,0:T(8,128)(2,1)}, bf16[960,256]{1,0:T(8,128)(2,1)S(1)}, u32[]{:S(2)}) copy-start(bf16[960,256]{1,0:T(8,128)(2,1)S(1)} %collective-permute-done.8.refs_4_) | copy-start | bytes 1474564
  55.6 2.8 %collective-permute-start.11 = (bf16[8,144,256]{2,1,0:T(8,128)(2,1)}, bf16[8,144,256]{2,1,0:T(8,128)(2,1)S(1)}, u32[]{:S(2)}, u32[]{:S(2)}) collective-permute-start(bf16[8,144,256]{2,1,0:T(8,128)(2,1)} %get-tuple-element.34), channel_id=1, source_target_pairs={{0,1},{1,0},{2,3},{3,2},{4,5},{5,4},{6,7},{7,6},{8,9},{9,8},{10,11... | collective-permute-start | bytes 1769480 | tf_op jit(solution)/shard_map/ppermute | solution.py:220
  55.7 4.4 %collective-permute-start.13 = (bf16[1440,256]{1,0:T(8,128)(2,1)S(1)}, bf16[1440,256]{1,0:T(8,128)(2,1)}, u32[]{:S(2)}, u32[]{:S(2)}) collective-permute-start(bf16[1440,256]{1,0:T(8,128)(2,1)S(1)} %bitcast.44), channel_id=1, source_target_pairs={{0,1},{1,0},{2,3},{3,2},{4,5},{5,4},{6,7},{7,6},{8,9},{9,8},{10,11... | collective-permute-start | bytes 2211848 | tf_op jit(solution)/shard_map/ppermute | solution.py:220
  57.3 2.8 %collective-permute-start.14 = (bf16[960,256]{1,0:T(8,128)(2,1)S(1)}, bf16[960,256]{1,0:T(8,128)(2,1)}, u32[]{:S(2)}, u32[]{:S(2)}) collective-permute-start(bf16[960,256]{1,0:T(8,128)(2,1)S(1)} %broadcast_select_fusion), channel_id=1, source_target_pairs={{0,1},{1,0},{2,3},{3,2},{4,5},{5,4},{6,7},{7,6},{8,9},{9,8},{10,11... | collective-permute-start | bytes 1474568 | tf_op jit(solution)/shard_map/ppermute | solution.py:220
  58.3 1.7 %collective-permute-start.15 = (bf16[480,256]{1,0:T(8,128)(2,1)S(1)}, bf16[480,256]{1,0:T(8,128)(2,1)S(1)}, u32[]{:S(2)}, u32[]{:S(2)}) collective-permute-start(bf16[480,256]{1,0:T(8,128)(2,1)S(1)} %broadcast_select_fusion.3), channel_id=1, source_target_pairs={{0,1},{1,0},{2,3},{3,2},{4,5},{5,4},{6,7},{7,6},{8,9},{9,8},{10,11... | collective-permute-start | bytes 737288 | tf_op jit(solution)/shard_map/ppermute | solution.py:220
  58.7 11.0 %collective-permute-start.12 = (bf16[4,144,256]{2,1,0:T(8,128)(2,1)S(1)}, bf16[4,144,256]{2,1,0:T(8,128)(2,1)S(1)}, u32[]{:S(2)}, u32[]{:S(2)}) collective-permute-start(bf16[4,144,256]{2,1,0:T(8,128)(2,1)S(1)} %dynamic-slice_bitcast_fusion), channel_id=1, source_target_pairs={{0,2},{1,3},{2,0},{3,1},{4,6},{5,7},{6,4},{7,5},{8,10},{9,11},{10,... | collective-permute-start | bytes 884744 | tf_op jit(solution)/shard_map/ppermute | solution.py:220
  60.1 0.7 copy-start.14
  69.8 6.3 %collective-permute-start.16 = (bf16[2,144,256]{2,1,0:T(8,128)(2,1)S(1)}, bf16[2,144,256]{2,1,0:T(8,128)(2,1)S(1)}, u32[]{:S(2)}, u32[]{:S(2)}) collective-permute-start(bf16[2,144,256]{2,1,0:T(8,128)(2,1)S(1)} %dynamic-slice_bitcast_fusion.1), channel_id=1, source_target_pairs={{0,4},{1,5},{2,6},{3,7},{4,0},{5,1},{6,2},{7,3},{8,12},{9,13},{10,... | collective-permute-start | bytes 442376 | tf_op jit(solution)/shard_map/ppermute | solution.py:220
  76.2 5.6 %collective-permute-start.17 = (bf16[1,144,256]{2,1,0:T(8,128)(2,1)S(1)}, bf16[1,144,256]{2,1,0:T(8,128)(2,1)S(1)}, u32[]{:S(2)}, u32[]{:S(2)}) collective-permute-start(bf16[1,144,256]{2,1,0:T(8,128)(2,1)S(1)} %constant_dynamic-slice_fusion), channel_id=1, source_target_pairs={{0,8},{1,9},{2,10},{3,11},{4,12},{5,13},{6,14},{7,15},{8,0},{9,1},... | collective-permute-start | bytes 221192 | tf_op jit(solution)/shard_map/ppermute | solution.py:220
